TPU v7x, 32 devices: a whole 2x2x4 slice. The times are simulated.
32 devices in a mesh: seq: 8 (over z, x), section: 2 (over core), dp: 2 (over y).
Axes of the slice: x: 2, y: 2, z: 4, core: 2. Of those that a mesh axis runs over, the one named last changes fastest.
Arguments:
- queries: bfloat16 [2, 1024, 3584], P('section', 'seq', 'dp'), may hold values from -5 to 5
- key_vectors: bfloat16 [2, 1024, 3584], P('section', 'seq', 'dp'), may hold values from -5 to 5
- value_vectors: bfloat16 [2, 1024, 3584], P('section', 'seq', 'dp'), may hold values from -6 to 6
- out_grad: bfloat16 [2, 1024, 3584], P('section', 'seq', 'dp'), may hold values from -6 to 6
- doc_lengths: int32 [8], replicated, may hold values from 1 to 384, 1024 in all
Outputs:
- query_grad: bfloat16 [2, 1024, 3584], P('section', 'seq', 'dp')
- key_grad: bfloat16 [2, 1024, 3584], P('section', 'seq', 'dp')
- value_grad: bfloat16 [2, 1024, 3584], P('section', 'seq', 'dp')
Inputs may be any that keep to these rules, and one draw needn't show every extreme that they name: `doc_lengths`: the 8 lengths sum to 1024; the longest is exactly 384.
All inputs are finite; a program needn't handle non-finite values.
Results may differ from a plain program's by a relative error of at most 0.024.
Values may be sent and summed in bfloat16 or wider, within the bound.
No kernel may reach another device: no remote copies, remote signals or barrier semaphores. Data moves between devices by JAX's collectives and lax.ppermute only.
A program may use at most 192 MiB of HBM per device.

v0:
```python
import functools
import math
import jax
import jax.numpy as jnp
from jax import lax
from jax.experimental import pallas as pl
from jax.experimental.pallas import tpu as pltpu
from jax.sharding import PartitionSpec as P

HEAD = 224
LANES = 128
FLOOR = -1e30


def pick_slot(stacked, slot):
    return lax.dynamic_index_in_dim(stacked, slot, 0, keepdims=False)


def put_slot(stacked, update, slot):
    return lax.dynamic_update_index_in_dim(stacked, update, slot, 0)


def spread_shards(queries, key_vectors, value_vectors, out_grad, doc_lengths):
    local_rows = queries.shape[1]
    local_width = queries.shape[2]
    head_count = local_width // HEAD
    seq_size = lax.axis_size("seq")
    group = seq_size // head_count
    scaling = HEAD ** (-0.5)

    def spread(matrix):
        shaped = matrix.reshape(local_rows, head_count, 1, HEAD)
        copies = jnp.broadcast_to(shaped, (local_rows, head_count, group, HEAD))
        return copies.reshape(local_rows, seq_size * HEAD)

    query_head, key_head, value_head, cot_head = (
        lax.all_to_all(spread(queries), "seq", split_axis=1, concat_axis=0, tiled=True),
        lax.all_to_all(spread(key_vectors), "seq", split_axis=1, concat_axis=0, tiled=True),
        lax.all_to_all(spread(value_vectors), "seq", split_axis=1, concat_axis=0, tiled=True),
        lax.all_to_all(spread(out_grad), "seq", split_axis=1, concat_axis=0, tiled=True),
    )
    length = key_head.shape[0]
    member = lax.axis_index("seq") % group
    blocks = 2 * group
    block = length // blocks
    bounds = jnp.cumsum(doc_lengths)
    positions = jnp.arange(length, dtype=jnp.int32)
    doc_index = jnp.sum((positions[:, None] >= bounds[None, :]).astype(jnp.int32), axis=1)
    row_list = [member, blocks - 1 - member]
    query_list = []
    cot_list = []
    pos_list = []
    for which in range(2):
        offset = row_list[which] * block
        query_list.append(lax.dynamic_slice_in_dim(query_head, offset, block, 0))
        cot_list.append(lax.dynamic_slice_in_dim(cot_head, offset, block, 0))
        pos_list.append(offset + jnp.arange(block, dtype=jnp.int32))
    query_stack = jnp.stack(query_list)
    cot_stack = jnp.stack(cot_list)
    pos_stack = jnp.stack(pos_list)
    doc_stack = jnp.take(doc_index, pos_stack)
    plan = []
    for number in range(blocks + 1):
        first = number <= member
        slot = jnp.where(first, 0, 1).astype(jnp.int32)
        col_block = jnp.where(first, number, number - member - 1)
        flag = None
        plan.append((slot, col_block, flag))
    row_max = jnp.full((2, block), -jnp.inf, jnp.float32)
    row_sum = jnp.zeros((2, block), jnp.float32)
    stored = []
    for slot, col_block, flag in plan:

        def score_tile(carry, slot=slot, col_block=col_block):
            maxima, totals = carry
            query_rows = pick_slot(query_stack, slot)
            key_rows = lax.dynamic_slice_in_dim(key_head, col_block * block, block, 0)
            col_docs = lax.dynamic_slice_in_dim(doc_index, col_block * block, block, 0)
            col_positions = col_block * block + jnp.arange(block, dtype=jnp.int32)
            raw = jnp.dot(query_rows, key_rows.T, preferred_element_type=jnp.float32) * scaling
            allowed = (pick_slot(doc_stack, slot)[:, None] == col_docs[None, :]) & (
                pick_slot(pos_stack, slot)[:, None] >= col_positions[None, :]
            )
            scores = jnp.where(allowed, raw, -jnp.inf)
            before = pick_slot(maxima, slot)
            after = jnp.maximum(before, jnp.max(scores, axis=1))
            safe = jnp.where(jnp.isfinite(after), after, 0.0)
            total = pick_slot(totals, slot) * jnp.exp(before - safe) + jnp.sum(
                jnp.exp(scores - safe[:, None]), axis=1
            )
            return (scores, put_slot(maxima, after, slot), put_slot(totals, total, slot))

        scores, row_max, row_sum = score_tile((row_max, row_sum))
        stored.append(scores)

    def tile_weights(scores, slot):
        return (
            jnp.exp(scores - pick_slot(row_max, slot)[:, None]) / pick_slot(row_sum, slot)[:, None]
        )

    summed = jnp.zeros((2, block, HEAD), jnp.float32)
    for (slot, col_block, flag), scores in zip(plan, stored):

        def add_values(carry, slot=slot, col_block=col_block, scores=scores):
            rounded = tile_weights(scores, slot).astype(jnp.bfloat16)
            value_rows = lax.dynamic_slice_in_dim(value_head, col_block * block, block, 0)
            term = jnp.dot(rounded, value_rows, preferred_element_type=jnp.float32)
            return put_slot(carry, pick_slot(carry, slot) + term, slot)

        summed = add_values(summed)
    attended = summed.astype(jnp.bfloat16)
    row_dot = jnp.sum(cot_stack.astype(jnp.float32) * attended.astype(jnp.float32), axis=2)
    query_acc = jnp.zeros((2, block, HEAD), jnp.float32)
    key_acc = jnp.zeros((length, HEAD), jnp.float32)
    value_acc = jnp.zeros((length, HEAD), jnp.float32)
    for (slot, col_block, flag), scores in zip(plan, stored):

        def backward_tile(carry, slot=slot, col_block=col_block, scores=scores):
            query_sum, key_sum, value_sum = carry
            weights = tile_weights(scores, slot)
            rounded = weights.astype(jnp.bfloat16)
            query_rows = pick_slot(query_stack, slot)
            cot_rows = pick_slot(cot_stack, slot)
            start = col_block * block
            key_rows = lax.dynamic_slice_in_dim(key_head, start, block, 0)
            value_rows = lax.dynamic_slice_in_dim(value_head, start, block, 0)
            value_term = jnp.dot(rounded.T, cot_rows, preferred_element_type=jnp.float32)
            prob_grad = jnp.dot(cot_rows, value_rows.T, preferred_element_type=jnp.float32)
            score_grad = (
                weights * (prob_grad - pick_slot(row_dot, slot)[:, None]) * scaling
            ).astype(jnp.bfloat16)
            query_term = jnp.dot(score_grad, key_rows, preferred_element_type=jnp.float32)
            key_term = jnp.dot(score_grad.T, query_rows, preferred_element_type=jnp.float32)
            query_sum = put_slot(query_sum, pick_slot(query_sum, slot) + query_term, slot)
            key_sum = lax.dynamic_update_slice_in_dim(
                key_sum, lax.dynamic_slice_in_dim(key_sum, start, block, 0) + key_term, start, 0
            )
            value_sum = lax.dynamic_update_slice_in_dim(
                value_sum,
                lax.dynamic_slice_in_dim(value_sum, start, block, 0) + value_term,
                start,
                0,
            )
            return (query_sum, key_sum, value_sum)

        query_acc, key_acc, value_acc = backward_tile((query_acc, key_acc, value_acc))
    query_rounded = query_acc.astype(jnp.bfloat16)
    key_back, value_back = (
        lax.all_to_all(key_acc, "seq", split_axis=0, concat_axis=1, tiled=True),
        lax.all_to_all(value_acc, "seq", split_axis=0, concat_axis=1, tiled=True),
    )

    def settle(received):
        shaped = received.astype(jnp.float32).reshape(local_rows, head_count, group, HEAD)
        return jnp.sum(shaped, axis=2).reshape(1, local_rows, local_width).astype(jnp.bfloat16)

    query_full = jnp.zeros((length, HEAD), jnp.bfloat16)
    for which in range(2):
        query_full = lax.dynamic_update_slice_in_dim(
            query_full, query_rounded[which], row_list[which] * block, 0
        )
    query_back = lax.all_to_all(query_full, "seq", split_axis=0, concat_axis=1, tiled=True)
    query_out = settle(query_back)
    return (query_out, settle(key_back), settle(value_back))


NT = ((1,), (1,))
NN = ((1,), (0,))
TN = ((0,), (0,))
GROUP = 8


def head_span(head):
    low = head * HEAD // LANES * LANES
    high = -(-(head + 1) * HEAD // LANES) * LANES
    return low, high


def head_mask(head):
    low, high = head_span(head)
    lane = lax.broadcasted_iota(jnp.int32, (1, high - low), 1) + low
    inside = (lane >= head * HEAD) & (lane < (head + 1) * HEAD)
    return inside.astype(jnp.float32).astype(jnp.bfloat16)


def matmul(left, right, dims):
    return lax.dot_general(left, right, (dims, ((), ())), preferred_element_type=jnp.float32)


def stack(values, axis):
    return values[0] if len(values) == 1 else jnp.concatenate(values, axis=axis)


def allowed(lengths_ref, rows, query_block, key_block):
    shape = (rows, rows)
    position = query_block * rows + lax.broadcasted_iota(jnp.int32, shape, 1)
    keys = key_block * rows + lax.broadcasted_iota(jnp.int32, shape, 0)
    start = jnp.zeros_like(position)
    bound = jnp.int32(0)
    for doc in range(1, lengths_ref.shape[0]):
        bound = bound + lengths_ref[doc]
        start = jnp.where(position >= bound, bound, start)
    return (keys >= start) & (keys <= position)


def make_tile(lengths_ref, rows, queries, keys):
    mask = stack(
        [stack([allowed(lengths_ref, rows, q, k) for _, q in queries], 1) for _, k in keys], 0
    )
    return [slot for slot, _ in queries], [slot for slot, _ in keys], mask


def tile_values(plan, head, queries, keys, products):
    low, high = head_span(head)
    keep = head_mask(head)

    def gather(refs, number, slots):
        return stack([refs[slot][number][0, :, low:high] for slot in slots], 0)

    out = []
    for query_slots, key_slots, _ in plan:
        q = [gather(queries, number, query_slots) for number in range(products)]
        k = [gather(keys, number, key_slots) * keep for number in range(products)]
        out.append((q, k, [matmul(b, a, NT) for a, b in zip(q, k)]))
    return out, keep


def tiles_ahead(heads, plan, queries, keys, products):
    yield from enumerate([tile_values(plan, head, queries, keys, products) for head in range(heads)])


def pair_tile(lengths_ref, rows, me, slots=(0, 1)):
    mate = me + 1 - 2 * lax.rem(me, 2)
    return make_tile(lengths_ref, rows, ((0, me), (1, mate)), [(slot, me - 2 * slot) for slot in slots])


def third_tile(third, lengths_ref, rows, me):
    slots, keys, mask = make_tile(lengths_ref, rows, ((2, me + 1),), ((1, me - 2),))
    return slots, keys, mask & (me == third)


def lane_cut(value, number, rows):
    return value[:, number * rows : (number + 1) * rows]


def row_of(group, kinds, kind, head):
    return pl.ds((group * kinds + kind) * GROUP + head, 1)


def per_query(slots, kinds, kind, head, ref):
    return stack([ref[row_of(slot, kinds, kind, head), :] for slot in slots], 1)


def collect_stats(heads, power, step, plan, queries, keys, rows, out_ref, groups):
    for head, (tiles, _) in tiles_ahead(heads, plan, queries, keys, 1):
        for (query_slots, _, mask), (_, _, (raw,)) in zip(plan, tiles):
            raw = jnp.where(mask, raw, FLOOR)
            top = jnp.max(raw, axis=0, keepdims=True)
            sums = jnp.sum(jnp.exp2((raw - top) * power), axis=0, keepdims=True)
            for number, slot in enumerate(query_slots):
                at = step * heads + head
                out_ref[row_of(groups[slot], 2, 0, at), :] = lane_cut(top, number, rows)
                out_ref[row_of(groups[slot], 2, 1, at), :] = lane_cut(sums, number, rows)


def stats_kernel(
    heads, power, place_ref, lengths_ref, q_own, q_mate, k_own, k_back, o_own, v_own, o_copy, v_copy, out_ref
):
    rows, me, step = k_own.shape[1], place_ref[0], place_ref[1]
    o_copy[...], v_copy[...] = o_own[...], v_own[...]
    plan = [pair_tile(lengths_ref, rows, me)]
    queries, keys = ((q_own,), (q_mate,)), ((k_own,), (k_back,))
    collect_stats(heads, power, step, plan, queries, keys, rows, out_ref, (0, 1))


def third_stats_kernel(third, heads, power, place_ref, lengths_ref, q_third, k_back, out_ref):
    rows, me, step = k_back.shape[1], place_ref[0], place_ref[1]
    plan = [third_tile(third, lengths_ref, rows, me)]
    queries, keys = (None, None, (q_third,)), (None, (k_back,))
    collect_stats(heads, power, step, plan, queries, keys, rows, out_ref, (None, None, 0))


def part_of(ref, kinds, number):
    size = kinds * GROUP
    return ref[number * size : (number + 1) * size, :]


def group_parts(kinds, mine, sent, extra):
    own = [part_of(mine, kinds, 0), part_of(sent, kinds, 1)]
    mate = [part_of(mine, kinds, 1), part_of(sent, kinds, 0)]
    if extra:
        near, far = extra
        own, mate = own + [near[...]], mate + [far[...]]
    return [own, mate]


def merge_groups(scaling, shift_ref, refs):
    mine, sent, *extra = refs
    for number, parts in enumerate(group_parts(2, mine, sent, extra)):
        shift_ref[number * GROUP : (number + 1) * GROUP, :] = merge_stats(scaling, parts)


def merge_stats(scaling, parts):
    split = [(jnp.where(p[GROUP:] > 0, p[:GROUP], FLOOR), p[GROUP:]) for p in parts]
    top = functools.reduce(jnp.maximum, [s[0] for s in split])
    total = sum(jnp.exp((s[0] - top) * scaling) * s[1] for s in split)
    return top + jnp.log(jnp.where(total > 0, total, 1.0)) / scaling


class Emitter:
    def __init__(self, outs, base={}):
        self.outs, self.base, self.carry = outs, base, {}

    def put(self, name, start, stop, value):
        if name in self.base:
            value = value + self.base[name][0, :, start:stop].astype(jnp.float32)
        self.outs[name][0, :, start:stop] = value.astype(jnp.bfloat16)

    def emit(self, head, name, value):
        low, high = head_span(head)
        first, last = head * HEAD % LANES == 0, (head + 1) * HEAD % LANES == 0
        start, stop = low, high
        if not first:
            self.put(name, low, low + LANES, value[:, :LANES] + self.carry.pop(name))
            start = low + LANES
        if not last:
            self.carry[name] = value[:, high - LANES - low :]
            stop = high - LANES
        if stop > start:
            self.put(name, start, stop, value[:, start - low : stop - low])


def add_rows(sums, kind, slots, value, rows):
    for number, slot in enumerate(slots):
        piece = value[number * rows : (number + 1) * rows]
        name = (kind, slot)
        sums[name] = sums[name] + piece if name in sums else piece


def split_refs(refs):
    return ((refs[0:2], refs[2:4]), (refs[4:6], refs[6:8]), refs[8:])


def values_kernel(merge, slots, heads, scaling, power, place_ref, lengths_ref, q0, o0, q1, o1, *refs):
    key_refs, refs = refs[: len(slots)], refs[len(slots) :]
    queries, keys = ((q0, o0), (q1, o1)), {slot: (ref,) for slot, ref in zip(slots, key_refs)}
    if merge:
        *refs, shift_ref = refs
        stats, value_refs = refs[: -len(slots)], refs[-len(slots) :]
        merge_groups(scaling, shift_ref, stats)
    else:
        shift_ref, value_refs = refs[0], refs[-len(slots) :]
    rows, me, step = q0.shape[1], place_ref[0], place_ref[1]
    plan = [pair_tile(lengths_ref, rows, me, slots)]
    out = Emitter({("v", slot): ref for slot, ref in zip(slots, value_refs)})
    weights = []
    for head, (tiles, keep) in tiles_ahead(heads, plan, queries, keys, 1):
        (query_slots, key_slots, mask), (_, _, (raw,)) = plan[0], tiles[0]
        shift = per_query(query_slots, 1, 0, step * heads + head, shift_ref)
        weight = jnp.where(mask, jnp.exp2((raw - shift) * power), 0.0)
        weights.append((weight.astype(jnp.bfloat16), keep))
    for head, (weight, keep) in enumerate(weights):
        low, high = head_span(head)
        o = stack([queries[slot][1][0, :, low:high] for slot in query_slots], 0) * keep
        sums = {}
        add_rows(sums, "v", key_slots, matmul(weight, o, NN), rows)
        for name, value in sums.items():
            out.emit(head, name, value)


def dots_kernel(merge, heads, scaling, power, place_ref, lengths_ref, *refs):
    queries, keys, refs = split_refs(refs)
    if merge:
        *stats, bundle_ref, dots_ref, shift_ref = refs
        merge_groups(scaling, shift_ref, stats)
        bundle_ref[: 4 * GROUP] = stats[0][...]
    else:
        shift_ref, dots_ref = refs
    rows, me, step = keys[0][0].shape[1], place_ref[0], place_ref[1]
    plan = [pair_tile(lengths_ref, rows, me)]
    for head, (tiles, _) in tiles_ahead(heads, plan, queries, keys, 2):
        at = step * heads + head
        for (query_slots, _, mask), (_, _, (raw, grads)) in zip(plan, tiles):
            shift = per_query(query_slots, 1, 0, at, shift_ref)
            weight = jnp.where(mask, jnp.exp2((raw - shift) * power), 0.0)
            dots = jnp.sum(weight * grads, axis=0, keepdims=True)
            for number, slot in enumerate(query_slots):
                dots_ref[row_of(slot, 1, 0, at), :] = lane_cut(dots, number, rows)
                if merge:
                    bundle_ref[row_of(4 + slot, 1, 0, at), :] = lane_cut(dots, number, rows)


def keys_kernel(third, heads, scaling, power, place_ref, lengths_ref, *refs):
    queries, keys, refs = split_refs(refs)
    (*base, shift_ref, mine, sent), refs = (refs[:3], refs[3:]) if third is None else (refs[:4], refs[4:])
    *extra, key_own, key_back, query_own, query_mate, total_ref = refs
    rows, me, step = keys[0][0].shape[1], place_ref[0], place_ref[1]
    plan = [pair_tile(lengths_ref, rows, me)]
    for number, parts in enumerate(group_parts(1, mine, sent, extra)):
        total_ref[number * GROUP : (number + 1) * GROUP, :] = sum(parts)
    outs = {("k", 0): key_own, ("k", 1): key_back, ("q", 0): query_own, ("q", 1): query_mate}
    out = Emitter(outs, {("k", 1): ref for ref in base})
    slopes = []
    for head, (tiles, keep) in tiles_ahead(heads, plan, queries, keys, 2):
        at = step * heads + head
        (query_slots, key_slots, mask), ((q, _), (k, _), (raw, grads)) = plan[0], tiles[0]
        shift = per_query(query_slots, 1, 0, at, shift_ref)
        dots = per_query(query_slots, 1, 0, at, total_ref)
        weight = jnp.where(mask, jnp.exp2((raw - shift) * power), 0.0)
        slope = (weight * (grads - dots) * scaling).astype(jnp.bfloat16)
        slopes.append((slope, q * keep, k))
    for head, (slope, q, k) in enumerate(slopes):
        sums = {}
        add_rows(sums, "k", key_slots, matmul(slope, q, NN), rows)
        add_rows(sums, "q", query_slots, matmul(slope, k, TN), rows)
        for name, value in sums.items():
            out.emit(head, name, value)


def third_kernel(
    third, heads, scaling, power, place_ref, lengths_ref, q_third, o_third, k_back, v_back, value_part,
    stats, even, odd, value_out, key_out, query_out, dots_ref, shift_ref,
):
    rows, me, step = k_back.shape[1], place_ref[0], place_ref[1]
    parts = [stats[...], part_of(even, 2, 0), part_of(odd, 2, 1)]
    shift_ref[...] = merge_stats(scaling, parts)
    slots, keys, mask = third_tile(third, lengths_ref, rows, me)
    queries, keys = (None, None, (q_third, o_third)), (None, (k_back, v_back))
    plan = [(slots, [1], mask)]
    out = Emitter({"v": value_out, "k": key_out, "q": query_out}, {"v": value_part})
    for head, (tiles, keep) in tiles_ahead(heads, plan, queries, keys, 2):
        (q, o), (k, _), (raw, grads) = tiles[0]
        at = step * heads + head
        weight = jnp.where(mask, jnp.exp2((raw - shift_ref[pl.ds(at, 1), :]) * power), 0.0)
        dots = jnp.sum(weight * grads, axis=0, keepdims=True)
        dots_ref[pl.ds(at, 1), :] = dots
        total = dots + even[row_of(4, 1, 0, at), :] + odd[row_of(5, 1, 0, at), :]
        slope = (weight * (grads - total) * scaling).astype(jnp.bfloat16)
        out.emit(head, "v", matmul(weight.astype(jnp.bfloat16), o * keep, NN))
        out.emit(head, "k", matmul(slope, q * keep, NN))
        out.emit(head, "q", matmul(slope, k, TN))


def add_refs(*refs):
    return sum(ref[...].astype(jnp.float32) for ref in refs)


def sums_kernel(key_part, key_sent, *refs):
    *query_parts, key_out, query_out = refs
    key_out[...] = add_refs(key_part, key_sent).astype(jnp.bfloat16)
    query_out[...] = add_refs(*query_parts).astype(jnp.bfloat16)


def halo_program(third, queries, key_vectors, value_vectors, out_grad, facts):
    _, rows, width = queries.shape
    seq_size = lax.axis_size("seq")
    me = lax.axis_index("seq").astype(jnp.int32)
    scaling = HEAD ** (-0.5)
    power = scaling * math.log2(math.e)
    steps = width // HEAD // 4
    part = width // steps
    heads = part // HEAD
    devices = range(seq_size)
    mates = [(s, s ^ 1) for s in devices]
    ring = third is None
    chain = [(s, s + 2) for s in devices if s + 2 < seq_size]
    ahead = [(s, (s + 2) % seq_size) for s in devices] if ring else chain
    behind = [(s, s - 2) for s in devices if s >= 2]
    if not ring:
        relay, to_odd = [(third + 2, third)], [(third, third + 2)]
        from_even, to_even = [(third + 1, third)], [(third, third + 1)]

    def send(value, pairs):
        return lax.ppermute(value, "seq", pairs)

    smem = pl.BlockSpec(memory_space=pltpu.SMEM)
    vmem = pl.BlockSpec(memory_space=pltpu.VMEM)
    wide_shape = jax.ShapeDtypeStruct((1, rows, width), jnp.bfloat16)

    def slim_shape(groups, kinds):
        return jax.ShapeDtypeStruct((groups * kinds * GROUP, rows), jnp.float32)

    def call(kernel, products, wides, slims, outs, slim_outs, plain=False, scratch=(), after=()):
        flops = 2 * products * 4 * rows * rows * width * 3 // 2
        lead = [] if plain else [me[None], facts]
        inputs = len(lead) + len(wides) + len(slims) + len(after)
        columns = {*range(len(lead), len(lead) + len(wides)), *range(inputs, inputs + outs)}

        def body(*refs):
            def half(step, carry):
                cut = pl.ds(pl.multiple_of(step * part, LANES), part)
                views = [ref.at[:, :, cut] if n in columns else ref for n, ref in enumerate(refs)]
                if not plain:
                    views[0] = (refs[0][0], step)
                kernel(*views)
                return carry

            lax.fori_loop(0, steps, half, 0)

        return pl.pallas_call(
            body,
            in_specs=[smem] * len(lead)
            + [vmem] * (len(wides) + len(slims))
            + [pl.BlockSpec(memory_space=pl.ANY)] * len(after),
            out_specs=[vmem] * (outs + len(slim_outs)),
            out_shape=[wide_shape] * outs + [slim_shape(*sizes) for sizes in slim_outs],
            scratch_shapes=[pltpu.VMEM((groups * GROUP, rows), jnp.float32) for groups in scratch],
            compiler_params=pltpu.CompilerParams(vmem_limit_bytes=20 * 1024 * 1024),
            cost_estimate=pl.CostEstimate(
                flops=flops, bytes_accessed=20 * rows * width, transcendentals=0
            ),
        )(*lead, *wides, *[value for _, _, value in slims], *after)

    query_mate = send(queries, mates)
    key_back = send(key_vectors, chain)
    grad_mate = send(out_grad, mates)
    value_back = send(value_vectors, ahead)
    grad_own, value_own, stats = call(
        functools.partial(stats_kernel, heads, power), 1,
        [queries, query_mate, key_vectors, key_back, out_grad, value_vectors], [], 2, [(2, 2)],
    )
    stats_mate = send(stats, mates)
    rows_in = [queries, grad_own, query_mate, grad_mate]
    tensors = rows_in + [key_vectors, value_own, key_back, value_back]
    constants = (heads, scaling, power)
    if ring:
        value_sent, shift = call(
            functools.partial(values_kernel, True, (1,), *constants), 1, rows_in + [key_back],
            [(2, 2, stats), (2, 2, stats_mate)], 1, [(2, 1)],
        )
        (dots,) = call(
            functools.partial(dots_kernel, False, *constants), 2, tensors, [(2, 1, shift)], 0, [(2, 1)]
        )
        dots_in = [(2, 1, shift), (2, 1, dots), (2, 1, send(dots, mates))]
        (value_part,) = call(
            functools.partial(values_kernel, False, (0,), *constants), 1, rows_in + [key_vectors],
            [(2, 1, shift)], 1, [], after=[dots],
        )
        base = []
    else:
        query_third = send(query_mate, relay)
        held, stats_mate = lax.optimization_barrier((grad_mate, stats_mate))
        grad_third = send(held, relay)
        query_third, _ = lax.optimization_barrier((query_third, value_back))
        (third_stats,) = call(
            functools.partial(third_stats_kernel, third, heads, power), 1, [query_third, key_back], [],
            0, [(1, 2)],
        )
        stats_in = [(2, 2, stats), (2, 2, stats_mate)]
        stats_in += [(1, 2, send(third_stats, to_even)), (1, 2, send(third_stats, to_odd))]
        bundle, dots, shift = call(
            functools.partial(dots_kernel, True, *constants), 2, tensors, stats_in, 0,
            [(2, 3), (2, 1), (2, 1)],
        )
        even, odd, dots_mate = send(bundle, from_even), send(bundle, relay), send(dots, mates)
        value_part, value_back_part = call(
            functools.partial(values_kernel, False, (0, 1), *constants), 2, rows_in + [key_vectors, key_back],
            [(2, 1, shift)], 2, [],
        )
        value_back_part, dots_mate = lax.optimization_barrier((value_back_part, dots_mate))
        value_sent, key_third, query_extra, third_dots = call(
            functools.partial(third_kernel, third, *constants), 2,
            [query_third, grad_third, key_back, value_back, value_back_part],
            [(1, 2, third_stats), (2, 3, even), (2, 3, odd)],
            3, [(1, 1)], scratch=[1],
        )
        dots_in = [(2, 1, shift), (2, 1, dots), (2, 1, dots_mate)]
        dots_in += [(1, 1, send(third_dots, to_even)), (1, 1, send(third_dots, to_odd))]
        base = [key_third]
    value_received = send(value_sent, behind)
    key_part, key_sent, query_part, query_sent = call(
        functools.partial(keys_kernel, third, *constants), 4, tensors + base, dots_in, 4, [], scratch=[2],
    )
    key_received = send(key_sent, behind)
    query_received = [send(query_sent, mates)] + ([] if ring else [send(query_extra, to_even)])
    value_ready = (value_part.astype(jnp.float32) + value_received.astype(jnp.float32)).astype(jnp.bfloat16)
    key_ready, query_ready = call(
        sums_kernel, 0, [key_part, key_received, query_part, *query_received], [], 2, [], plain=True
    )
    return query_ready, key_ready, value_ready


def program_kernel(shift, lengths_ref, out_ref):
    start, found = jnp.int32(0), jnp.int32(0)
    for doc in range(lengths_ref.shape[0]):
        end = start + lengths_ref[doc]
        last = (end - 1) >> shift
        spans = (last - (start >> shift) >= 3) & (last & 1 == 0)
        found = jnp.where(spans, (last >> 1) - 1, found)
        out_ref[doc + 1] = lengths_ref[doc]
        start = end
    out_ref[0] = found


def program_facts(rows, doc_lengths):
    smem = pl.BlockSpec(memory_space=pltpu.SMEM)
    return pl.pallas_call(
        functools.partial(program_kernel, rows.bit_length() - 1),
        in_specs=[smem],
        out_specs=smem,
        out_shape=jax.ShapeDtypeStruct((doc_lengths.shape[0] + 1,), jnp.int32),
    )(doc_lengths)


def halo_shards(*arguments):
    *tensors, doc_lengths = arguments
    facts = program_facts(tensors[0].shape[1], doc_lengths)
    thirds = range(3, lax.axis_size("seq") - 2, 2)
    programs = [functools.partial(halo_program, third) for third in (None, *thirds)]
    return lax.switch(facts[0], programs, *tensors, facts)


def shards(queries, key_vectors, value_vectors, out_grad, doc_lengths):
    _, rows, width = queries.shape
    seq_size = lax.axis_size("seq")
    longest = rows * seq_size * 3 // 8
    fits = longest <= 3 * rows and seq_size % 2 == 0 and seq_size > 4 and rows == LANES
    heads = width // HEAD
    plan = halo_shards if fits and heads % 4 == 0 and heads <= GROUP else spread_shards
    return plan(queries, key_vectors, value_vectors, out_grad, doc_lengths)


def solution(mesh):
    return jax.shard_map(
        shards,
        mesh=mesh,
        in_specs=(
            P("section", "seq", "dp"),
            P("section", "seq", "dp"),
            P("section", "seq", "dp"),
            P("section", "seq", "dp"),
            P(),
        ),
        out_specs=(P("section", "seq", "dp"), P("section", "seq", "dp"), P("section", "seq", "dp")),
        check_vma=False,
    )
```

profile of v0, /device:TPU:0, one launch (start us, length us, event | category | flops | bytes accessed | tf_op | source)
XLA Modules:
  0.0 52.0 jit_solution(16440375854665461748)
XLA Ops:
  0.6 1.3 %shard_map.91 = s32[9]{0:T(128)S(1)} custom-call(s32[8]{0:T(128)} %lengths_ref.1), custom_call_target="tpu_custom_call" | custom-call | tf_op jit(solution)/shard_map/pallas_call | solution.py:597
  2.0 50.0 %conditional.4 = (bf16[1,128,1792]{2,1,0:T(8,128)(2,1)}, bf16[1,128,1792]{2,1,0:T(8,128)(2,1)}, bf16[1,128,1792]{2,1,0:T(8,128)(2,1)}) conditional(s32[]{:T(128)} %bitcast.3, (bf16[1,128,1792]{2,1,0:T(8,128)(2,1)}, bf16[1,128,1792]{2,1,0:T(8,128)(2,1)}, s32[9]{0:T(128)S(1)}, bf16[1,128,1792]{2,1,0:T(8,128)(2,1)}, ...), branch_computations={%region_0.0_spmd, %region_1.0_spmd, %region_2.0_spmd} | conditional | flops 4228775936 | bytes 55903040
  2.0 3.0 %collective-permute-start = (bf16[1,128,1792]{2,1,0:T(8,128)(2,1)}, bf16[1,128,1792]{2,1,0:T(8,128)(2,1)S(1)}, u32[]{:S(2)}, u32[]{:S(2)}) collective-permute-start(bf16[1,128,1792]{2,1,0:T(8,128)(2,1)} %get-tuple-element.128.refs_2_), channel_id=1, source_target_pairs={{0,4},{4,0},{8,12},{12,8},{16,20},{20,16},{24,28},{28,24},{1,5},{5... | collective-permute-start | bytes 1376264 | tf_op jit(solution)/shard_map/cond/branch_0_fun/ppermute | solution.py:474
  5.0 3.5 %collective-permute-start.1 = (bf16[1,128,1792]{2,1,0:T(8,128)(2,1)}, bf16[1,128,1792]{2,1,0:T(8,128)(2,1)S(1)}, u32[]{:S(2)}, u32[]{:S(2)}) collective-permute-start(bf16[1,128,1792]{2,1,0:T(8,128)(2,1)} %get-tuple-element.131.refs_4_.refs_6_), channel_id=1, source_target_pairs={{0,8},{4,12},{8,16},{12,20},{16,24},{20,28},{1,9},{5,13},{9,17},{1... | collective-permute-start | bytes 1376264 | tf_op jit(solution)/shard_map/cond/branch_0_fun/ppermute | solution.py:474
  8.5 0.6 %collective-permute-start.2 = (bf16[1,128,1792]{2,1,0:T(8,128)(2,1)}, bf16[1,128,1792]{2,1,0:T(8,128)(2,1)S(1)}, u32[]{:S(2)}, u32[]{:S(2)}) collective-permute-start(bf16[1,128,1792]{2,1,0:T(8,128)(2,1)} %get-tuple-element.134.refs_6_), channel_id=1, source_target_pairs={{0,4},{4,0},{8,12},{12,8},{16,20},{20,16},{24,28},{28,24},{1,5},{5... | collective-permute-start | bytes 1376264 | tf_op jit(solution)/shard_map/cond/branch_0_fun/ppermute | solution.py:474
  9.1 1.6 %collective-permute-start.3 = (bf16[1,128,1792]{2,1,0:T(8,128)(2,1)}, bf16[1,128,1792]{2,1,0:T(8,128)(2,1)S(1)}, u32[]{:S(2)}, u32[]{:S(2)}) collective-permute-start(bf16[1,128,1792]{2,1,0:T(8,128)(2,1)} %get-tuple-element.137.refs_7_), channel_id=1, source_target_pairs={{0,8},{4,12},{8,16},{12,20},{16,24},{20,28},{24,0},{28,4},{1,9},{5... | collective-permute-start | bytes 1376264 | tf_op jit(solution)/shard_map/cond/branch_0_fun/ppermute | solution.py:474
  10.6 5.9 %collective-permute-done.refs_3_.refs_4_ = bf16[1,128,1792]{2,1,0:T(8,128)(2,1)S(1)} collective-permute-done((bf16[1,128,1792]{2,1,0:T(8,128)(2,1)}, bf16[1,128,1792]{2,1,0:T(8,128)(2,1)S(1)}, u32[]{:S(2)}, u32[]{:S(2)}) %collective-permute-start) | collective-permute-done | bytes 458784 | tf_op jit(solution)/shard_map/cond/branch_0_fun/ppermute | solution.py:474
  16.5 3.2 %collective-permute-done.1.refs_5_.refs_6_.refs_8_ = bf16[1,128,1792]{2,1,0:T(8,128)(2,1)S(1)} collective-permute-done((bf16[1,128,1792]{2,1,0:T(8,128)(2,1)}, bf16[1,128,1792]{2,1,0:T(8,128)(2,1)S(1)}, u32[]{:S(2)}, u32[]{:S(2)}) %collective-permute-start.1) | collective-permute-done | bytes 458784 | tf_op jit(solution)/shard_map/cond/branch_0_fun/ppermute | solution.py:474
  19.7 2.6 %branch_0_fun.6 = (bf16[1,128,1792]{2,1,0:T(8,128)(2,1)S(1)}, bf16[1,128,1792]{2,1,0:T(8,128)(2,1)S(1)}, f32[32,128]{1,0:T(8,128)S(1)}) custom-call(s32[1]{0:T(128)} %bitcast.refs_0_, s32[9]{0:T(128)S(1)} %get-tuple-element.40.refs_1_, bf16[1,128,1792]{2,1,0:T(8,128)(2,1)} %get-tuple-element.128.refs_2_, ...), custom_call_target="tpu_custom_call" | custom-call | flops 352321536 | bytes 4587520 | tf_op jit(solution)/shard_map/cond/branch_0_fun/pallas_call | solution.py:500
  22.4 0.6 %collective-permute-start.4 = (f32[32,128]{1,0:T(8,128)S(1)}, f32[32,128]{1,0:T(8,128)S(1)}, u32[]{:S(2)}, u32[]{:S(2)}) collective-permute-start(f32[32,128]{1,0:T(8,128)S(1)} %get-tuple-element.47.refs_7_), channel_id=1, source_target_pairs={{0,4},{4,0},{8,12},{12,8},{16,20},{20,16},{24,28},{28,24},{1,5},{5... | collective-permute-start | bytes 49160 | tf_op jit(solution)/shard_map/cond/branch_0_fun/ppermute | solution.py:474
  23.0 2.8 %collective-permute-done.2.refs_5_ = bf16[1,128,1792]{2,1,0:T(8,128)(2,1)S(1)} collective-permute-done((bf16[1,128,1792]{2,1,0:T(8,128)(2,1)}, bf16[1,128,1792]{2,1,0:T(8,128)(2,1)S(1)}, u32[]{:S(2)}, u32[]{:S(2)}) %collective-permute-start.2) | collective-permute-done | bytes 458784 | tf_op jit(solution)/shard_map/cond/branch_0_fun/ppermute | solution.py:474
  26.2 1.6 %branch_0_fun.7 = (bf16[1,128,1792]{2,1,0:T(8,128)(2,1)S(1)}, f32[16,128]{1,0:T(8,128)S(1)}) custom-call(s32[1]{0:T(128)} %bitcast.refs_0_, s32[9]{0:T(128)S(1)} %get-tuple-element.40.refs_1_, bf16[1,128,1792]{2,1,0:T(8,128)(2,1)S(1)} %copy-done, bf16[1,128,1792]{2,1,0:T(8,128)(2,1)S(1)} %get-tuple-element.45.refs_3_, ...), custom_call_target="tpu_custom_call" | custom-call | flops 352321536 | bytes 4587520 | tf_op jit(solution)/shard_map/cond/branch_0_fun/pallas_call | solution.py:500
  27.7 1.3 %collective-permute-start.8 = (bf16[1,128,1792]{2,1,0:T(8,128)(2,1)S(1)}, bf16[1,128,1792]{2,1,0:T(8,128)(2,1)S(1)}, u32[]{:S(2)}, u32[]{:S(2)}) collective-permute-start(bf16[1,128,1792]{2,1,0:T(8,128)(2,1)S(1)} %get-tuple-element.55), channel_id=1, source_target_pairs={{8,0},{12,4},{16,8},{20,12},{24,16},{28,20},{9,1},{13,5},{17,9},{2... | collective-permute-start | bytes 1376264 | tf_op jit(solution)/shard_map/cond/branch_0_fun/ppermute | solution.py:474
  29.1 1.9 %branch_0_fun.8.refs_11_.refs_8_ = f32[16,128]{1,0:T(8,128)S(1)} custom-call(s32[1]{0:T(128)} %bitcast.refs_0_, s32[9]{0:T(128)S(1)} %get-tuple-element.40.refs_1_, bf16[1,128,1792]{2,1,0:T(8,128)(2,1)S(1)} %copy-done, bf16[1,128,1792]{2,1,0:T(8,128)(2,1)S(1)} %get-tuple-element.45.refs_3_, bf16[1,128,1792]{2,1,0:T(8,128)(2,1)S(1)} %collective-permute-done.refs_3_.refs_4_, ...), custom_call_target="tpu_custom_call" | custom-call | flops 704643072 | bytes 4587520 | tf_op jit(solution)/shard_map/cond/branch_0_fun/pallas_call | solution.py:500
  30.9 1.5 %collective-permute-start.5 = (f32[16,128]{1,0:T(8,128)S(1)}, f32[16,128]{1,0:T(8,128)S(1)}, u32[]{:S(2)}, u32[]{:S(2)}) collective-permute-start(f32[16,128]{1,0:T(8,128)S(1)} %branch_0_fun.8.refs_11_.refs_8_), channel_id=1, source_target_pairs={{0,4},{4,0},{8,12},{12,8},{16,20},{20,16},{24,28},{28,24},{1,5},{5... | collective-permute-start | bytes 24584 | tf_op jit(solution)/shard_map/cond/branch_0_fun/ppermute | solution.py:474
  32.5 1.6 %branch_0_fun.11 = bf16[1,128,1792]{2,1,0:T(8,128)(2,1)S(1)} custom-call(s32[1]{0:T(128)} %bitcast.refs_0_, s32[9]{0:T(128)S(1)} %get-tuple-element.40.refs_1_, bf16[1,128,1792]{2,1,0:T(8,128)(2,1)S(1)} %copy-done, bf16[1,128,1792]{2,1,0:T(8,128)(2,1)S(1)} %get-tuple-element.45.refs_3_, bf16[1,128,1792]{2,1,0:T(8,128)(2,1)S(1)} %collective-permute-done.refs_3_.refs_4_, ...), custom_call_target="tpu_custom_call" | custom-call | flops 352321536 | bytes 4587520 | tf_op jit(solution)/shard_map/cond/branch_0_fun/pallas_call | solution.py:500
  34.0 0.6 %collective-permute-done.5.refs_12_ = f32[16,128]{1,0:T(8,128)S(1)} collective-permute-done((f32[16,128]{1,0:T(8,128)S(1)}, f32[16,128]{1,0:T(8,128)S(1)}, u32[]{:S(2)}, u32[]{:S(2)}) %collective-permute-start.5) | collective-permute-done | bytes 8224 | tf_op jit(solution)/shard_map/cond/branch_0_fun/ppermute | solution.py:474
  34.6 2.7 %branch_0_fun.9 = (bf16[1,128,1792]{2,1,0:T(8,128)(2,1)S(1)}, bf16[1,128,1792]{2,1,0:T(8,128)(2,1)S(1)}, bf16[1,128,1792]{2,1,0:T(8,128)(2,1)S(1)}, bf16[1,128,1792]{2,1,0:T(8,128)(2,1)S(1)}) custom-call(s32[1]{0:T(128)} %bitcast.refs_0_, s32[9]{0:T(128)S(1)} %get-tuple-element.40.refs_1_, bf16[1,128,1792]{2,1,0:T(8,128)(2,1)S(1)} %copy-done, ...), custom_call_target="tpu_custom_call" | custom-call | flops 1409286144 | bytes 4587520 | tf_op jit(solution)/shard_map/cond/branch_0_fun/pallas_call | solution.py:500
  37.4 1.3 %collective-permute-start.6 = (bf16[1,128,1792]{2,1,0:T(8,128)(2,1)S(1)}, bf16[1,128,1792]{2,1,0:T(8,128)(2,1)S(1)}, u32[]{:S(2)}, u32[]{:S(2)}) collective-permute-start(bf16[1,128,1792]{2,1,0:T(8,128)(2,1)S(1)} %get-tuple-element.50), channel_id=1, source_target_pairs={{8,0},{12,4},{16,8},{20,12},{24,16},{28,20},{9,1},{13,5},{17,9},{2... | collective-permute-start | bytes 1376264 | tf_op jit(solution)/shard_map/cond/branch_0_fun/ppermute | solution.py:474
  38.7 1.6 %collective-permute-start.7 = (bf16[1,128,1792]{2,1,0:T(8,128)(2,1)S(1)}, bf16[1,128,1792]{2,1,0:T(8,128)(2,1)S(1)}, u32[]{:S(2)}, u32[]{:S(2)}) collective-permute-start(bf16[1,128,1792]{2,1,0:T(8,128)(2,1)S(1)} %get-tuple-element.52), channel_id=1, source_target_pairs={{0,4},{4,0},{8,12},{12,8},{16,20},{20,16},{24,28},{28,24},{1,5},{5... | collective-permute-start | bytes 1376264 | tf_op jit(solution)/shard_map/cond/branch_0_fun/ppermute | solution.py:474
  40.2 1.3 %collective-permute-done.8 = bf16[1,128,1792]{2,1,0:T(8,128)(2,1)S(1)} collective-permute-done((bf16[1,128,1792]{2,1,0:T(8,128)(2,1)S(1)}, bf16[1,128,1792]{2,1,0:T(8,128)(2,1)S(1)}, u32[]{:S(2)}, u32[]{:S(2)}) %collective-permute-start.8) | collective-permute-done | bytes 458784 | tf_op jit(solution)/shard_map/cond/branch_0_fun/ppermute | solution.py:474
  41.5 0.9 %convert_add_fusion = bf16[1,128,1792]{2,1,0:T(8,128)(2,1)} fusion(bf16[1,128,1792]{2,1,0:T(8,128)(2,1)S(1)} %collective-permute-done.8, bf16[1,128,1792]{2,1,0:T(8,128)(2,1)S(1)} %branch_0_fun.11), kind=kLoop, calls=%fused_computation | loop fusion | flops 917504 | bytes 1376256 | tf_op jit(solution)/shard_map/cond/branch_0_fun/add | solution.py:576
  42.4 8.5 %collective-permute-done.6.refs_1_ = bf16[1,128,1792]{2,1,0:T(8,128)(2,1)S(1)} collective-permute-done((bf16[1,128,1792]{2,1,0:T(8,128)(2,1)S(1)}, bf16[1,128,1792]{2,1,0:T(8,128)(2,1)S(1)}, u32[]{:S(2)}, u32[]{:S(2)}) %collective-permute-start.6) | collective-permute-done | bytes 458784 | tf_op jit(solution)/shard_map/cond/branch_0_fun/ppermute | solution.py:474
  50.9 1.1 %branch_0_fun.10 = (bf16[1,128,1792]{2,1,0:T(8,128)(2,1)}, bf16[1,128,1792]{2,1,0:T(8,128)(2,1)}) custom-call(bf16[1,128,1792]{2,1,0:T(8,128)(2,1)S(1)} %get-tuple-element.49.refs_0_, bf16[1,128,1792]{2,1,0:T(8,128)(2,1)S(1)} %collective-permute-done.6.refs_1_, bf16[1,128,1792]{2,1,0:T(8,128)(2,1)S(1)} %get-tuple-element.51.refs_2_, ...), custom_call_target="tpu_custom_call" | custom-call | bytes 4587520 | tf_op jit(solution)/shard_map/cond/branch_0_fun/pallas_call | solution.py:500
  (7 shorter events, 0.5 us)
Async XLA Ops:
  2.0 14.6 %collective-permute-start = (bf16[1,128,1792]{2,1,0:T(8,128)(2,1)}, bf16[1,128,1792]{2,1,0:T(8,128)(2,1)S(1)}, u32[]{:S(2)}, u32[]{:S(2)}) collective-permute-start(bf16[1,128,1792]{2,1,0:T(8,128)(2,1)} %get-tuple-element.128.refs_2_), channel_id=1, source_target_pairs={{0,4},{4,0},{8,12},{12,8},{16,20},{20,16},{24,28},{28,24},{1,5},{5... | collective-permute-start | bytes 1376264 | tf_op jit(solution)/shard_map/cond/branch_0_fun/ppermute | solution.py:474
  5.0 14.7 %collective-permute-start.1 = (bf16[1,128,1792]{2,1,0:T(8,128)(2,1)}, bf16[1,128,1792]{2,1,0:T(8,128)(2,1)S(1)}, u32[]{:S(2)}, u32[]{:S(2)}) collective-permute-start(bf16[1,128,1792]{2,1,0:T(8,128)(2,1)} %get-tuple-element.131.refs_4_.refs_6_), channel_id=1, source_target_pairs={{0,8},{4,12},{8,16},{12,20},{16,24},{20,28},{1,9},{5,13},{9,17},{1... | collective-permute-start | bytes 1376264 | tf_op jit(solution)/shard_map/cond/branch_0_fun/ppermute | solution.py:474
  8.5 17.2 %collective-permute-start.2 = (bf16[1,128,1792]{2,1,0:T(8,128)(2,1)}, bf16[1,128,1792]{2,1,0:T(8,128)(2,1)S(1)}, u32[]{:S(2)}, u32[]{:S(2)}) collective-permute-start(bf16[1,128,1792]{2,1,0:T(8,128)(2,1)} %get-tuple-element.134.refs_6_), channel_id=1, source_target_pairs={{0,4},{4,0},{8,12},{12,8},{16,20},{20,16},{24,28},{28,24},{1,5},{5... | collective-permute-start | bytes 1376264 | tf_op jit(solution)/shard_map/cond/branch_0_fun/ppermute | solution.py:474
  9.1 20.0 %collective-permute-start.3 = (bf16[1,128,1792]{2,1,0:T(8,128)(2,1)}, bf16[1,128,1792]{2,1,0:T(8,128)(2,1)S(1)}, u32[]{:S(2)}, u32[]{:S(2)}) collective-permute-start(bf16[1,128,1792]{2,1,0:T(8,128)(2,1)} %get-tuple-element.137.refs_7_), channel_id=1, source_target_pairs={{0,8},{4,12},{8,16},{12,20},{16,24},{20,28},{24,0},{28,4},{1,9},{5... | collective-permute-start | bytes 1376264 | tf_op jit(solution)/shard_map/cond/branch_0_fun/ppermute | solution.py:474
  19.7 6.4 %copy-start = (bf16[1,128,1792]{2,1,0:T(8,128)(2,1)S(1)}, bf16[1,128,1792]{2,1,0:T(8,128)(2,1)}, u32[]{:S(2)}) copy-start(bf16[1,128,1792]{2,1,0:T(8,128)(2,1)} %get-tuple-element.128.refs_2_) | copy-start | bytes 1376260
  22.4 3.8 %collective-permute-start.4 = (f32[32,128]{1,0:T(8,128)S(1)}, f32[32,128]{1,0:T(8,128)S(1)}, u32[]{:S(2)}, u32[]{:S(2)}) collective-permute-start(f32[32,128]{1,0:T(8,128)S(1)} %get-tuple-element.47.refs_7_), channel_id=1, source_target_pairs={{0,4},{4,0},{8,12},{12,8},{16,20},{20,16},{24,28},{28,24},{1,5},{5... | collective-permute-start | bytes 49160 | tf_op jit(solution)/shard_map/cond/branch_0_fun/ppermute | solution.py:474
  26.2 2.9 %copy-start.3 = (bf16[1,128,1792]{2,1,0:T(8,128)(2,1)S(1)}, bf16[1,128,1792]{2,1,0:T(8,128)(2,1)}, u32[]{:S(2)}) copy-start(bf16[1,128,1792]{2,1,0:T(8,128)(2,1)} %get-tuple-element.131.refs_4_.refs_6_) | copy-start | bytes 1376260
  27.7 13.8 %collective-permute-start.8 = (bf16[1,128,1792]{2,1,0:T(8,128)(2,1)S(1)}, bf16[1,128,1792]{2,1,0:T(8,128)(2,1)S(1)}, u32[]{:S(2)}, u32[]{:S(2)}) collective-permute-start(bf16[1,128,1792]{2,1,0:T(8,128)(2,1)S(1)} %get-tuple-element.55), channel_id=1, source_target_pairs={{8,0},{12,4},{16,8},{20,12},{24,16},{28,20},{9,1},{13,5},{17,9},{2... | collective-permute-start | bytes 1376264 | tf_op jit(solution)/shard_map/cond/branch_0_fun/ppermute | solution.py:474
  30.9 3.7 %collective-permute-start.5 = (f32[16,128]{1,0:T(8,128)S(1)}, f32[16,128]{1,0:T(8,128)S(1)}, u32[]{:S(2)}, u32[]{:S(2)}) collective-permute-start(f32[16,128]{1,0:T(8,128)S(1)} %branch_0_fun.8.refs_11_.refs_8_), channel_id=1, source_target_pairs={{0,4},{4,0},{8,12},{12,8},{16,20},{20,16},{24,28},{28,24},{1,5},{5... | collective-permute-start | bytes 24584 | tf_op jit(solution)/shard_map/cond/branch_0_fun/ppermute | solution.py:474
  37.4 13.5 %collective-permute-start.6 = (bf16[1,128,1792]{2,1,0:T(8,128)(2,1)S(1)}, bf16[1,128,1792]{2,1,0:T(8,128)(2,1)S(1)}, u32[]{:S(2)}, u32[]{:S(2)}) collective-permute-start(bf16[1,128,1792]{2,1,0:T(8,128)(2,1)S(1)} %get-tuple-element.50), channel_id=1, source_target_pairs={{8,0},{12,4},{16,8},{20,12},{24,16},{28,20},{9,1},{13,5},{17,9},{2... | collective-permute-start | bytes 1376264 | tf_op jit(solution)/shard_map/cond/branch_0_fun/ppermute | solution.py:474
  38.7 12.3 %collective-permute-start.7 = (bf16[1,128,1792]{2,1,0:T(8,128)(2,1)S(1)}, bf16[1,128,1792]{2,1,0:T(8,128)(2,1)S(1)}, u32[]{:S(2)}, u32[]{:S(2)}) collective-permute-start(bf16[1,128,1792]{2,1,0:T(8,128)(2,1)S(1)} %get-tuple-element.52), channel_id=1, source_target_pairs={{0,4},{4,0},{8,12},{12,8},{16,20},{20,16},{24,28},{28,24},{1,5},{5... | collective-permute-start | bytes 1376264 | tf_op jit(solution)/shard_map/cond/branch_0_fun/ppermute | solution.py:474
where the time goes:
time: 52.2 us; the launch traced here: 52 us
  waiting for transfers between devices  22.7 us (43%)
  starting transfers between devices  14.9 us (29%)
  Pallas kernels  12.7 us (24%)
  other arithmetic  0.91 us (2%)
  between operations  0.67 us (1%)
    ppermute x9, waiting for transfers between devices, send(): return lax.ppermute(value, 'seq', pairs)  22.7 us
    ppermute x9, starting transfers between devices, send(): return lax.ppermute(value, 'seq', pairs)  14.9 us
    pallas_call x6, Pallas kernels, call(): pl.pallas_call(body, in_specs=[smem] * len(lead) + [vmem] * (len(wides) +...  11.4 us
    pallas_call x1, Pallas kernels, program_facts(): pl.pallas_call(functools.partial(program_kernel, rows.bit_length() - 1),...  1.29 us
  transfers between devices with their start and end apart: 9, of which 7 were waited for; matrix products, arithmetic and copies ran while one was open for 2% of the time, Pallas kernels for 20%

commit v1 on v0

--- a/solution.py
+++ b/solution.py
@@ -192,9 +192,8 @@
 
 
 def allowed(lengths_ref, rows, query_block, key_block):
-    shape = (rows, rows)
-    position = query_block * rows + lax.broadcasted_iota(jnp.int32, shape, 1)
-    keys = key_block * rows + lax.broadcasted_iota(jnp.int32, shape, 0)
+    position = query_block * rows + lax.broadcasted_iota(jnp.int32, (1, rows), 1)
+    keys = key_block * rows + lax.broadcasted_iota(jnp.int32, (rows, rows), 0)
     start = jnp.zeros_like(position)
     bound = jnp.int32(0)
     for doc in range(1, lengths_ref.shape[0]):

time: 52.2 us -> 73.9 us (1.42)
  the two profiles are of different devices: /device:TPU:0 before, /device:TPU:16 now
where the time goes in v1:
time: 73.9 us; the launch traced here: 73.6 us
  waiting for transfers between devices  32.1 us (43%)
  starting transfers between devices  25.3 us (34%)
  Pallas kernels  14.4 us (19%)
  other arithmetic  0.87 us (1%)
    ppermute x18, waiting for transfers between devices, send(): return lax.ppermute(value, 'seq', pairs)  32.1 us
    ppermute x18, starting transfers between devices, send(): return lax.ppermute(value, 'seq', pairs)  25.3 us
    pallas_call x7, Pallas kernels, call(): pl.pallas_call(body, in_specs=[smem] * len(lead) + [vmem] * (len(wides) +...  13.1 us
  transfers between devices with their start and end apart: 18, of which 11 were waited for; matrix products, arithmetic and copies ran while one was open for 1% of the time, Pallas kernels for 14%

profile of v1, /device:TPU:16, one launch (start us, length us, event | category | flops | bytes accessed | tf_op | source)
XLA Modules:
  0.0 73.6 jit_solution(16440375854665461748)
XLA Ops:
  0.6 1.3 %shard_map.91 = s32[9]{0:T(128)S(1)} custom-call(s32[8]{0:T(128)} %lengths_ref.1), custom_call_target="tpu_custom_call" | custom-call | tf_op jit(solution)/shard_map/pallas_call | solution.py:596
  2.0 71.6 %conditional.4 = (bf16[1,128,1792]{2,1,0:T(8,128)(2,1)}, bf16[1,128,1792]{2,1,0:T(8,128)(2,1)}, bf16[1,128,1792]{2,1,0:T(8,128)(2,1)}) conditional(s32[]{:T(128)} %bitcast.3, (bf16[1,128,1792]{2,1,0:T(8,128)(2,1)}, bf16[1,128,1792]{2,1,0:T(8,128)(2,1)}, s32[9]{0:T(128)S(1)}, bf16[1,128,1792]{2,1,0:T(8,128)(2,1)}, ...), branch_computations={%region_0.0_spmd, %region_1.0_spmd, %region_2.0_spmd} | conditional | flops 4228775936 | bytes 55903040
  2.0 1.6 %collective-permute-start.9 = (bf16[1,128,1792]{2,1,0:T(8,128)(2,1)}, bf16[1,128,1792]{2,1,0:T(8,128)(2,1)S(1)}, u32[]{:S(2)}, u32[]{:S(2)}) collective-permute-start(bf16[1,128,1792]{2,1,0:T(8,128)(2,1)} %get-tuple-element.129.refs_2_), channel_id=1, source_target_pairs={{0,4},{4,0},{8,12},{12,8},{16,20},{20,16},{24,28},{28,24},{1,5},{5... | collective-permute-start | bytes 1376264 | tf_op jit(solution)/shard_map/cond/branch_1_fun/ppermute | solution.py:473
  3.5 3.5 %collective-permute-start.10 = (bf16[1,128,1792]{2,1,0:T(8,128)(2,1)}, bf16[1,128,1792]{2,1,0:T(8,128)(2,1)S(1)}, u32[]{:S(2)}, u32[]{:S(2)}) collective-permute-start(bf16[1,128,1792]{2,1,0:T(8,128)(2,1)} %get-tuple-element.132.refs_4_.refs_6_), channel_id=1, source_target_pairs={{0,8},{4,12},{8,16},{12,20},{16,24},{20,28},{1,9},{5,13},{9,17},{1... | collective-permute-start | bytes 1376264 | tf_op jit(solution)/shard_map/cond/branch_1_fun/ppermute | solution.py:473
  7.6 1.9 %collective-permute-start.12 = (bf16[1,128,1792]{2,1,0:T(8,128)(2,1)}, bf16[1,128,1792]{2,1,0:T(8,128)(2,1)S(1)}, u32[]{:S(2)}, u32[]{:S(2)}) collective-permute-start(bf16[1,128,1792]{2,1,0:T(8,128)(2,1)} %get-tuple-element.138.refs_7_), channel_id=1, source_target_pairs={{0,8},{4,12},{8,16},{12,20},{16,24},{20,28},{1,9},{5,13},{9,17},{1... | collective-permute-start | bytes 1376264 | tf_op jit(solution)/shard_map/cond/branch_1_fun/ppermute | solution.py:473
  9.5 6.1 %collective-permute-done.9.refs_3_.refs_4_ = bf16[1,128,1792]{2,1,0:T(8,128)(2,1)S(1)} collective-permute-done((bf16[1,128,1792]{2,1,0:T(8,128)(2,1)}, bf16[1,128,1792]{2,1,0:T(8,128)(2,1)S(1)}, u32[]{:S(2)}, u32[]{:S(2)}) %collective-permute-start.9) | collective-permute-done | bytes 458784 | tf_op jit(solution)/shard_map/cond/branch_1_fun/ppermute | solution.py:473
  16.4 2.7 %collective-permute-done.10.refs_5_.refs_3_.refs_8_.refs_7_.refs_4_ = bf16[1,128,1792]{2,1,0:T(8,128)(2,1)S(1)} collective-permute-done((bf16[1,128,1792]{2,1,0:T(8,128)(2,1)}, bf16[1,128,1792]{2,1,0:T(8,128)(2,1)S(1)}, u32[]{:S(2)}, u32[]{:S(2)}) %collective-permute-start.10) | collective-permute-done | bytes 458784 | tf_op jit(solution)/shard_map/cond/branch_1_fun/ppermute | solution.py:473
  19.1 2.6 %branch_1_fun.7 = (bf16[1,128,1792]{2,1,0:T(8,128)(2,1)S(1)}, bf16[1,128,1792]{2,1,0:T(8,128)(2,1)S(1)}, f32[32,128]{1,0:T(8,128)S(1)}) custom-call(s32[1]{0:T(128)} %bitcast.1.refs_0_, s32[9]{0:T(128)S(1)} %get-tuple-element.56.refs_1_, bf16[1,128,1792]{2,1,0:T(8,128)(2,1)} %get-tuple-element.129.refs_2_, ...), custom_call_target="tpu_custom_call" | custom-call | flops 352321536 | bytes 4587520 | tf_op jit(solution)/shard_map/cond/branch_1_fun/pallas_call | solution.py:499
  22.3 2.2 %collective-permute-done.11.refs_5_ = bf16[1,128,1792]{2,1,0:T(8,128)(2,1)S(1)} collective-permute-done((bf16[1,128,1792]{2,1,0:T(8,128)(2,1)}, bf16[1,128,1792]{2,1,0:T(8,128)(2,1)S(1)}, u32[]{:S(2)}, u32[]{:S(2)}) %collective-permute-start.11) | collective-permute-done | bytes 458784 | tf_op jit(solution)/shard_map/cond/branch_1_fun/ppermute | solution.py:473
  28.6 1.3 %collective-permute-start.16 = (f32[16,128]{1,0:T(8,128)S(1)}, f32[16,128]{1,0:T(8,128)S(1)}, u32[]{:S(2)}, u32[]{:S(2)}) collective-permute-start(f32[16,128]{1,0:T(8,128)S(1)} %branch_1_fun.8.refs_7_), channel_id=1, source_target_pairs={{12,16},{13,17},{14,18},{15,19}} | collective-permute-start | bytes 24584 | tf_op jit(solution)/shard_map/cond/branch_1_fun/ppermute | solution.py:473
  30.6 4.5 %collective-permute-done.16.refs_12_ = f32[16,128]{1,0:T(8,128)S(1)} collective-permute-done((f32[16,128]{1,0:T(8,128)S(1)}, f32[16,128]{1,0:T(8,128)S(1)}, u32[]{:S(2)}, u32[]{:S(2)}) %collective-permute-start.16) | collective-permute-done | bytes 8224 | tf_op jit(solution)/shard_map/cond/branch_1_fun/ppermute | solution.py:473
  35.1 1.9 %branch_1_fun.9 = (f32[48,128]{1,0:T(8,128)S(1)}, f32[16,128]{1,0:T(8,128)S(1)}, f32[16,128]{1,0:T(8,128)S(1)}) custom-call(s32[1]{0:T(128)} %bitcast.1.refs_0_, s32[9]{0:T(128)S(1)} %get-tuple-element.56.refs_1_, bf16[1,128,1792]{2,1,0:T(8,128)(2,1)S(1)} %copy-done.1, bf16[1,128,1792]{2,1,0:T(8,128)(2,1)S(1)} %get-tuple-element.61.refs_3_, ...), custom_call_target="tpu_custom_call" | custom-call | flops 704643072 | bytes 4587520 | tf_op jit(solution)/shard_map/cond/branch_1_fun/pallas_call | solution.py:499
  37.0 2.9 %collective-permute-start.19 = (f32[48,128]{1,0:T(8,128)S(1)}, f32[48,128]{1,0:T(8,128)S(1)}, u32[]{:S(2)}, u32[]{:S(2)}) collective-permute-start(f32[48,128]{1,0:T(8,128)S(1)} %get-tuple-element.71), channel_id=1, source_target_pairs={{16,12},{17,13},{18,14},{19,15}} | collective-permute-start | bytes 73736 | tf_op jit(solution)/shard_map/cond/branch_1_fun/ppermute | solution.py:473
  41.8 1.8 %branch_1_fun.10 = (bf16[1,128,1792]{2,1,0:T(8,128)(2,1)S(1)}, bf16[1,128,1792]{2,1,0:T(8,128)(2,1)S(1)}) custom-call(s32[1]{0:T(128)} %bitcast.1.refs_0_, s32[9]{0:T(128)S(1)} %get-tuple-element.56.refs_1_, bf16[1,128,1792]{2,1,0:T(8,128)(2,1)S(1)} %copy-done.1, bf16[1,128,1792]{2,1,0:T(8,128)(2,1)S(1)} %get-tuple-element.61.refs_3_, ...), custom_call_target="tpu_custom_call" | custom-call | flops 704643072 | bytes 4587520 | tf_op jit(solution)/shard_map/cond/branch_1_fun/pallas_call | solution.py:499
  44.3 1.9 %branch_1_fun.11 = (bf16[1,128,1792]{2,1,0:T(8,128)(2,1)S(1)}, bf16[1,128,1792]{2,1,0:T(8,128)(2,1)S(1)}, bf16[1,128,1792]{2,1,0:T(8,128)(2,1)S(1)}, f32[8,128]{1,0:T(8,128)S(1)}) custom-call(s32[1]{0:T(128)} %bitcast.1.refs_0_, s32[9]{0:T(128)S(1)} %get-tuple-element.56.refs_1_, bf16[1,128,1792]{2,1,0:T(8,128)(2,1)S(1)} %collective-permute-done.13.refs_2_, ...), custom_call_target="tpu_custom_call" | custom-call | flops 704643072 | bytes 4587520 | tf_op jit(solution)/shard_map/cond/branch_1_fun/pallas_call | solution.py:499
  46.2 1.9 %collective-permute-start.26 = (bf16[1,128,1792]{2,1,0:T(8,128)(2,1)S(1)}, bf16[1,128,1792]{2,1,0:T(8,128)(2,1)S(1)}, u32[]{:S(2)}, u32[]{:S(2)}) collective-permute-start(bf16[1,128,1792]{2,1,0:T(8,128)(2,1)S(1)} %get-tuple-element.83), channel_id=1, source_target_pairs={{8,0},{12,4},{16,8},{20,12},{24,16},{28,20},{9,1},{13,5},{17,9},{2... | collective-permute-start | bytes 1376264 | tf_op jit(solution)/shard_map/cond/branch_1_fun/ppermute | solution.py:473
  48.1 1.3 %collective-permute-start.21 = (f32[8,128]{1,0:T(8,128)S(1)}, f32[8,128]{1,0:T(8,128)S(1)}, u32[]{:S(2)}, u32[]{:S(2)}) collective-permute-start(f32[8,128]{1,0:T(8,128)S(1)} %get-tuple-element.74), channel_id=1, source_target_pairs={{12,16},{13,17},{14,18},{15,19}} | collective-permute-start | bytes 12296 | tf_op jit(solution)/shard_map/cond/branch_1_fun/ppermute | solution.py:473
  50.1 1.3 %collective-permute-start.25 = (bf16[1,128,1792]{2,1,0:T(8,128)(2,1)S(1)}, bf16[1,128,1792]{2,1,0:T(8,128)(2,1)S(1)}, u32[]{:S(2)}, u32[]{:S(2)}) collective-permute-start(bf16[1,128,1792]{2,1,0:T(8,128)(2,1)S(1)} %get-tuple-element.79), channel_id=1, source_target_pairs={{12,16},{13,17},{14,18},{15,19}} | collective-permute-start | bytes 1376264 | tf_op jit(solution)/shard_map/cond/branch_1_fun/ppermute | solution.py:473
  51.4 3.2 %collective-permute-done.21.refs_14_ = f32[8,128]{1,0:T(8,128)S(1)} collective-permute-done((f32[8,128]{1,0:T(8,128)S(1)}, f32[8,128]{1,0:T(8,128)S(1)}, u32[]{:S(2)}, u32[]{:S(2)}) %collective-permute-start.21) | collective-permute-done | bytes 4128 | tf_op jit(solution)/shard_map/cond/branch_1_fun/ppermute | solution.py:473
  54.6 2.7 %branch_1_fun.12 = (bf16[1,128,1792]{2,1,0:T(8,128)(2,1)S(1)}, bf16[1,128,1792]{2,1,0:T(8,128)(2,1)S(1)}, bf16[1,128,1792]{2,1,0:T(8,128)(2,1)S(1)}, bf16[1,128,1792]{2,1,0:T(8,128)(2,1)S(1)}) custom-call(s32[1]{0:T(128)} %bitcast.1.refs_0_, s32[9]{0:T(128)S(1)} %get-tuple-element.56.refs_1_, bf16[1,128,1792]{2,1,0:T(8,128)(2,1)S(1)} %copy-done.1, ...), custom_call_target="tpu_custom_call" | custom-call | flops 1409286144 | bytes 4587520 | tf_op jit(solution)/shard_map/cond/branch_1_fun/pallas_call | solution.py:499
  57.3 1.9 %collective-permute-start.23 = (bf16[1,128,1792]{2,1,0:T(8,128)(2,1)S(1)}, bf16[1,128,1792]{2,1,0:T(8,128)(2,1)S(1)}, u32[]{:S(2)}, u32[]{:S(2)}) collective-permute-start(bf16[1,128,1792]{2,1,0:T(8,128)(2,1)S(1)} %get-tuple-element.76), channel_id=1, source_target_pairs={{8,0},{12,4},{16,8},{20,12},{24,16},{28,20},{9,1},{13,5},{17,9},{2... | collective-permute-start | bytes 1376264 | tf_op jit(solution)/shard_map/cond/branch_1_fun/ppermute | solution.py:473
  59.3 1.9 %collective-permute-start.24 = (bf16[1,128,1792]{2,1,0:T(8,128)(2,1)S(1)}, bf16[1,128,1792]{2,1,0:T(8,128)(2,1)S(1)}, u32[]{:S(2)}, u32[]{:S(2)}) collective-permute-start(bf16[1,128,1792]{2,1,0:T(8,128)(2,1)S(1)} %get-tuple-element.78), channel_id=1, source_target_pairs={{0,4},{4,0},{8,12},{12,8},{16,20},{20,16},{24,28},{28,24},{1,5},{5... | collective-permute-start | bytes 1376264 | tf_op jit(solution)/shard_map/cond/branch_1_fun/ppermute | solution.py:473
  62.7 5.0 %collective-permute-done.23.refs_1_ = bf16[1,128,1792]{2,1,0:T(8,128)(2,1)S(1)} collective-permute-done((bf16[1,128,1792]{2,1,0:T(8,128)(2,1)S(1)}, bf16[1,128,1792]{2,1,0:T(8,128)(2,1)S(1)}, u32[]{:S(2)}, u32[]{:S(2)}) %collective-permute-start.23) | collective-permute-done | bytes 458784 | tf_op jit(solution)/shard_map/cond/branch_1_fun/ppermute | solution.py:473
  67.7 4.7 %collective-permute-done.24.refs_3_ = bf16[1,128,1792]{2,1,0:T(8,128)(2,1)S(1)} collective-permute-done((bf16[1,128,1792]{2,1,0:T(8,128)(2,1)S(1)}, bf16[1,128,1792]{2,1,0:T(8,128)(2,1)S(1)}, u32[]{:S(2)}, u32[]{:S(2)}) %collective-permute-start.24) | collective-permute-done | bytes 458784 | tf_op jit(solution)/shard_map/cond/branch_1_fun/ppermute | solution.py:473
  (26 shorter events, 12.5 us)
Async XLA Ops:
  2.0 13.7 %collective-permute-start.9 = (bf16[1,128,1792]{2,1,0:T(8,128)(2,1)}, bf16[1,128,1792]{2,1,0:T(8,128)(2,1)S(1)}, u32[]{:S(2)}, u32[]{:S(2)}) collective-permute-start(bf16[1,128,1792]{2,1,0:T(8,128)(2,1)} %get-tuple-element.129.refs_2_), channel_id=1, source_target_pairs={{0,4},{4,0},{8,12},{12,8},{16,20},{20,16},{24,28},{28,24},{1,5},{5... | collective-permute-start | bytes 1376264 | tf_op jit(solution)/shard_map/cond/branch_1_fun/ppermute | solution.py:473
  3.5 15.5 %collective-permute-start.10 = (bf16[1,128,1792]{2,1,0:T(8,128)(2,1)}, bf16[1,128,1792]{2,1,0:T(8,128)(2,1)S(1)}, u32[]{:S(2)}, u32[]{:S(2)}) collective-permute-start(bf16[1,128,1792]{2,1,0:T(8,128)(2,1)} %get-tuple-element.132.refs_4_.refs_6_), channel_id=1, source_target_pairs={{0,8},{4,12},{8,16},{12,20},{16,24},{20,28},{1,9},{5,13},{9,17},{1... | collective-permute-start | bytes 1376264 | tf_op jit(solution)/shard_map/cond/branch_1_fun/ppermute | solution.py:473
  7.0 17.5 %collective-permute-start.11 = (bf16[1,128,1792]{2,1,0:T(8,128)(2,1)}, bf16[1,128,1792]{2,1,0:T(8,128)(2,1)S(1)}, u32[]{:S(2)}, u32[]{:S(2)}) collective-permute-start(bf16[1,128,1792]{2,1,0:T(8,128)(2,1)} %get-tuple-element.135.refs_6_), channel_id=1, source_target_pairs={{0,4},{4,0},{8,12},{12,8},{16,20},{20,16},{24,28},{28,24},{1,5},{5... | collective-permute-start | bytes 1376264 | tf_op jit(solution)/shard_map/cond/branch_1_fun/ppermute | solution.py:473
  7.6 19.8 %collective-permute-start.12 = (bf16[1,128,1792]{2,1,0:T(8,128)(2,1)}, bf16[1,128,1792]{2,1,0:T(8,128)(2,1)S(1)}, u32[]{:S(2)}, u32[]{:S(2)}) collective-permute-start(bf16[1,128,1792]{2,1,0:T(8,128)(2,1)} %get-tuple-element.138.refs_7_), channel_id=1, source_target_pairs={{0,8},{4,12},{8,16},{12,20},{16,24},{20,28},{1,9},{5,13},{9,17},{1... | collective-permute-start | bytes 1376264 | tf_op jit(solution)/shard_map/cond/branch_1_fun/ppermute | solution.py:473
  15.7 11.8 %collective-permute-start.13 = (bf16[1,128,1792]{2,1,0:T(8,128)(2,1)S(1)}, bf16[1,128,1792]{2,1,0:T(8,128)(2,1)S(1)}, u32[]{:S(2)}, u32[]{:S(2)}) collective-permute-start(bf16[1,128,1792]{2,1,0:T(8,128)(2,1)S(1)} %collective-permute-done.9.refs_3_.refs_4_), channel_id=1, source_target_pairs={{20,12},{21,13},{22,14},{23,15}} | collective-permute-start | bytes 1376264 | tf_op jit(solution)/shard_map/cond/branch_1_fun/ppermute | solution.py:473
  21.7 13.4 %copy-start.1 = (bf16[1,128,1792]{2,1,0:T(8,128)(2,1)S(1)}, bf16[1,128,1792]{2,1,0:T(8,128)(2,1)}, u32[]{:S(2)}) copy-start(bf16[1,128,1792]{2,1,0:T(8,128)(2,1)} %get-tuple-element.129.refs_2_) | copy-start | bytes 1376260
  21.7 13.4 %copy-start.4 = (bf16[1,128,1792]{2,1,0:T(8,128)(2,1)S(1)}, bf16[1,128,1792]{2,1,0:T(8,128)(2,1)}, u32[]{:S(2)}) copy-start(bf16[1,128,1792]{2,1,0:T(8,128)(2,1)} %get-tuple-element.132.refs_4_.refs_6_) | copy-start | bytes 1376260
  21.7 3.8 %collective-permute-start.14 = (f32[32,128]{1,0:T(8,128)S(1)}, f32[32,128]{1,0:T(8,128)S(1)}, u32[]{:S(2)}, u32[]{:S(2)}) collective-permute-start(f32[32,128]{1,0:T(8,128)S(1)} %get-tuple-element.64.refs_10_), channel_id=1, source_target_pairs={{0,4},{4,0},{8,12},{12,8},{16,20},{20,16},{24,28},{28,24},{1,5},{5... | collective-permute-start | bytes 49160 | tf_op jit(solution)/shard_map/cond/branch_1_fun/ppermute | solution.py:473
  25.5 18.8 %collective-permute-start.15 = (bf16[1,128,1792]{2,1,0:T(8,128)(2,1)S(1)}, bf16[1,128,1792]{2,1,0:T(8,128)(2,1)S(1)}, u32[]{:S(2)}, u32[]{:S(2)}) collective-permute-start(bf16[1,128,1792]{2,1,0:T(8,128)(2,1)S(1)} %collective-permute-done.11.refs_5_), channel_id=1, source_target_pairs={{20,12},{21,13},{22,14},{23,15}} | collective-permute-start | bytes 1376264 | tf_op jit(solution)/shard_map/cond/branch_1_fun/ppermute | solution.py:473
  28.6 6.4 %collective-permute-start.16 = (f32[16,128]{1,0:T(8,128)S(1)}, f32[16,128]{1,0:T(8,128)S(1)}, u32[]{:S(2)}, u32[]{:S(2)}) collective-permute-start(f32[16,128]{1,0:T(8,128)S(1)} %branch_1_fun.8.refs_7_), channel_id=1, source_target_pairs={{12,16},{13,17},{14,18},{15,19}} | collective-permute-start | bytes 24584 | tf_op jit(solution)/shard_map/cond/branch_1_fun/ppermute | solution.py:473
  29.9 5.1 %collective-permute-start.17 = (f32[16,128]{1,0:T(8,128)S(1)}, f32[16,128]{1,0:T(8,128)S(1)}, u32[]{:S(2)}, u32[]{:S(2)}) collective-permute-start(f32[16,128]{1,0:T(8,128)S(1)} %branch_1_fun.8.refs_7_), channel_id=1, source_target_pairs={{12,20},{13,21},{14,22},{15,23}} | collective-permute-start | bytes 24584 | tf_op jit(solution)/shard_map/cond/branch_1_fun/ppermute | solution.py:473
  37.0 7.3 %collective-permute-start.19 = (f32[48,128]{1,0:T(8,128)S(1)}, f32[48,128]{1,0:T(8,128)S(1)}, u32[]{:S(2)}, u32[]{:S(2)}) collective-permute-start(f32[48,128]{1,0:T(8,128)S(1)} %get-tuple-element.71), channel_id=1, source_target_pairs={{16,12},{17,13},{18,14},{19,15}} | collective-permute-start | bytes 73736 | tf_op jit(solution)/shard_map/cond/branch_1_fun/ppermute | solution.py:473
  39.9 4.4 %collective-permute-start.20 = (f32[48,128]{1,0:T(8,128)S(1)}, f32[48,128]{1,0:T(8,128)S(1)}, u32[]{:S(2)}, u32[]{:S(2)}) collective-permute-start(f32[48,128]{1,0:T(8,128)S(1)} %get-tuple-element.71), channel_id=1, source_target_pairs={{20,12},{21,13},{22,14},{23,15}} | collective-permute-start | bytes 73736 | tf_op jit(solution)/shard_map/cond/branch_1_fun/ppermute | solution.py:473
  40.6 3.7 %collective-permute-start.18 = (f32[16,128]{1,0:T(8,128)S(1)}, f32[16,128]{1,0:T(8,128)S(1)}, u32[]{:S(2)}, u32[]{:S(2)}) collective-permute-start(f32[16,128]{1,0:T(8,128)S(1)} %get-tuple-element.69.refs_12_), channel_id=1, source_target_pairs={{0,4},{4,0},{8,12},{12,8},{16,20},{20,16},{24,28},{28,24},{1,5},{5... | collective-permute-start | bytes 24584 | tf_op jit(solution)/shard_map/cond/branch_1_fun/ppermute | solution.py:473
  46.2 15.0 %collective-permute-start.26 = (bf16[1,128,1792]{2,1,0:T(8,128)(2,1)S(1)}, bf16[1,128,1792]{2,1,0:T(8,128)(2,1)S(1)}, u32[]{:S(2)}, u32[]{:S(2)}) collective-permute-start(bf16[1,128,1792]{2,1,0:T(8,128)(2,1)S(1)} %get-tuple-element.83), channel_id=1, source_target_pairs={{8,0},{12,4},{16,8},{20,12},{24,16},{28,20},{9,1},{13,5},{17,9},{2... | collective-permute-start | bytes 1376264 | tf_op jit(solution)/shard_map/cond/branch_1_fun/ppermute | solution.py:473
  48.1 6.5 %collective-permute-start.21 = (f32[8,128]{1,0:T(8,128)S(1)}, f32[8,128]{1,0:T(8,128)S(1)}, u32[]{:S(2)}, u32[]{:S(2)}) collective-permute-start(f32[8,128]{1,0:T(8,128)S(1)} %get-tuple-element.74), channel_id=1, source_target_pairs={{12,16},{13,17},{14,18},{15,19}} | collective-permute-start | bytes 12296 | tf_op jit(solution)/shard_map/cond/branch_1_fun/ppermute | solution.py:473
  49.4 5.2 %collective-permute-start.22 = (f32[8,128]{1,0:T(8,128)S(1)}, f32[8,128]{1,0:T(8,128)S(1)}, u32[]{:S(2)}, u32[]{:S(2)}) collective-permute-start(f32[8,128]{1,0:T(8,128)S(1)} %get-tuple-element.74), channel_id=1, source_target_pairs={{12,20},{13,21},{14,22},{15,23}} | collective-permute-start | bytes 12296 | tf_op jit(solution)/shard_map/cond/branch_1_fun/ppermute | solution.py:473
  50.1 12.6 %collective-permute-start.25 = (bf16[1,128,1792]{2,1,0:T(8,128)(2,1)S(1)}, bf16[1,128,1792]{2,1,0:T(8,128)(2,1)S(1)}, u32[]{:S(2)}, u32[]{:S(2)}) collective-permute-start(bf16[1,128,1792]{2,1,0:T(8,128)(2,1)S(1)} %get-tuple-element.79), channel_id=1, source_target_pairs={{12,16},{13,17},{14,18},{15,19}} | collective-permute-start | bytes 1376264 | tf_op jit(solution)/shard_map/cond/branch_1_fun/ppermute | solution.py:473
  57.3 10.4 %collective-permute-start.23 = (bf16[1,128,1792]{2,1,0:T(8,128)(2,1)S(1)}, bf16[1,128,1792]{2,1,0:T(8,128)(2,1)S(1)}, u32[]{:S(2)}, u32[]{:S(2)}) collective-permute-start(bf16[1,128,1792]{2,1,0:T(8,128)(2,1)S(1)} %get-tuple-element.76), channel_id=1, source_target_pairs={{8,0},{12,4},{16,8},{20,12},{24,16},{28,20},{9,1},{13,5},{17,9},{2... | collective-permute-start | bytes 1376264 | tf_op jit(solution)/shard_map/cond/branch_1_fun/ppermute | solution.py:473
  59.3 13.2 %collective-permute-start.24 = (bf16[1,128,1792]{2,1,0:T(8,128)(2,1)S(1)}, bf16[1,128,1792]{2,1,0:T(8,128)(2,1)S(1)}, u32[]{:S(2)}, u32[]{:S(2)}) collective-permute-start(bf16[1,128,1792]{2,1,0:T(8,128)(2,1)S(1)} %get-tuple-element.78), channel_id=1, source_target_pairs={{0,4},{4,0},{8,12},{12,8},{16,20},{20,16},{24,28},{28,24},{1,5},{5... | collective-permute-start | bytes 1376264 | tf_op jit(solution)/shard_map/cond/branch_1_fun/ppermute | solution.py:473

commit v2 on v1

--- a/solution.py
+++ b/solution.py
@@ -487,14 +487,19 @@
 
         def body(*refs):
             def half(step, carry):
-                cut = pl.ds(pl.multiple_of(step * part, LANES), part)
+                start = step * part
+                cut = pl.ds(start if ring else pl.multiple_of(start, LANES), part)
                 views = [ref.at[:, :, cut] if n in columns else ref for n, ref in enumerate(refs)]
                 if not plain:
                     views[0] = (refs[0][0], step)
                 kernel(*views)
                 return carry
 
-            lax.fori_loop(0, steps, half, 0)
+            if ring:
+                for step in range(steps):
+                    half(step, 0)
+            else:
+                lax.fori_loop(0, steps, half, 0)
 
         return pl.pallas_call(
             body,

time: 73.9 us -> 52 us (0.70)
  the two profiles are of different devices: /device:TPU:16 before, /device:TPU:0 now
where the time goes in v2:
time: 52 us; the launch traced here: 51.8 us
  waiting for transfers between devices  23.1 us (44%)
  starting transfers between devices  15.3 us (29%)
  Pallas kernels  11.7 us (22%)
  other arithmetic  0.91 us (2%)
  between operations  0.67 us (1%)
    ppermute x9, waiting for transfers between devices, send(): return lax.ppermute(value, 'seq', pairs)  23.1 us
    ppermute x9, starting transfers between devices, send(): return lax.ppermute(value, 'seq', pairs)  15.3 us
    pallas_call x6, Pallas kernels, call(): pl.pallas_call(body, in_specs=[smem] * len(lead) + [vmem] * (len(wides) +...  10.4 us
    pallas_call x1, Pallas kernels, program_facts(): pl.pallas_call(functools.partial(program_kernel, rows.bit_length() - 1),...  1.29 us
  transfers between devices with their start and end apart: 9, of which 7 were waited for; matrix products, arithmetic and copies ran while one was open for 2% of the time, Pallas kernels for 18%

profile of v2, /device:TPU:0, one launch (start us, length us, event | category | flops | bytes accessed | tf_op | source)
XLA Modules:
  0.0 51.8 jit_solution(14988001764243760282)
XLA Ops:
  0.6 1.3 %shard_map.91 = s32[9]{0:T(128)S(1)} custom-call(s32[8]{0:T(128)} %lengths_ref.1), custom_call_target="tpu_custom_call" | custom-call | tf_op jit(solution)/shard_map/pallas_call | solution.py:601
  2.0 49.8 %conditional.4 = (bf16[1,128,1792]{2,1,0:T(8,128)(2,1)}, bf16[1,128,1792]{2,1,0:T(8,128)(2,1)}, bf16[1,128,1792]{2,1,0:T(8,128)(2,1)}) conditional(s32[]{:T(128)} %bitcast.3, (bf16[1,128,1792]{2,1,0:T(8,128)(2,1)}, bf16[1,128,1792]{2,1,0:T(8,128)(2,1)}, s32[9]{0:T(128)S(1)}, bf16[1,128,1792]{2,1,0:T(8,128)(2,1)}, ...), branch_computations={%region_0.0_spmd, %region_1.0_spmd, %region_2.0_spmd} | conditional | flops 4228775936 | bytes 55903040
  2.0 3.0 %collective-permute-start = (bf16[1,128,1792]{2,1,0:T(8,128)(2,1)}, bf16[1,128,1792]{2,1,0:T(8,128)(2,1)S(1)}, u32[]{:S(2)}, u32[]{:S(2)}) collective-permute-start(bf16[1,128,1792]{2,1,0:T(8,128)(2,1)} %get-tuple-element.128.refs_2_), channel_id=1, source_target_pairs={{0,4},{4,0},{8,12},{12,8},{16,20},{20,16},{24,28},{28,24},{1,5},{5... | collective-permute-start | bytes 1376264 | tf_op jit(solution)/shard_map/cond/branch_0_fun/ppermute | solution.py:473
  5.0 3.5 %collective-permute-start.1 = (bf16[1,128,1792]{2,1,0:T(8,128)(2,1)}, bf16[1,128,1792]{2,1,0:T(8,128)(2,1)S(1)}, u32[]{:S(2)}, u32[]{:S(2)}) collective-permute-start(bf16[1,128,1792]{2,1,0:T(8,128)(2,1)} %get-tuple-element.131.refs_4_.refs_6_), channel_id=1, source_target_pairs={{0,8},{4,12},{8,16},{12,20},{16,24},{20,28},{1,9},{5,13},{9,17},{1... | collective-permute-start | bytes 1376264 | tf_op jit(solution)/shard_map/cond/branch_0_fun/ppermute | solution.py:473
  8.5 0.6 %collective-permute-start.2 = (bf16[1,128,1792]{2,1,0:T(8,128)(2,1)}, bf16[1,128,1792]{2,1,0:T(8,128)(2,1)S(1)}, u32[]{:S(2)}, u32[]{:S(2)}) collective-permute-start(bf16[1,128,1792]{2,1,0:T(8,128)(2,1)} %get-tuple-element.134.refs_6_), channel_id=1, source_target_pairs={{0,4},{4,0},{8,12},{12,8},{16,20},{20,16},{24,28},{28,24},{1,5},{5... | collective-permute-start | bytes 1376264 | tf_op jit(solution)/shard_map/cond/branch_0_fun/ppermute | solution.py:473
  9.1 1.6 %collective-permute-start.3 = (bf16[1,128,1792]{2,1,0:T(8,128)(2,1)}, bf16[1,128,1792]{2,1,0:T(8,128)(2,1)S(1)}, u32[]{:S(2)}, u32[]{:S(2)}) collective-permute-start(bf16[1,128,1792]{2,1,0:T(8,128)(2,1)} %get-tuple-element.137.refs_7_), channel_id=1, source_target_pairs={{0,8},{4,12},{8,16},{12,20},{16,24},{20,28},{24,0},{28,4},{1,9},{5... | collective-permute-start | bytes 1376264 | tf_op jit(solution)/shard_map/cond/branch_0_fun/ppermute | solution.py:473
  10.6 5.9 %collective-permute-done.refs_3_.refs_4_ = bf16[1,128,1792]{2,1,0:T(8,128)(2,1)S(1)} collective-permute-done((bf16[1,128,1792]{2,1,0:T(8,128)(2,1)}, bf16[1,128,1792]{2,1,0:T(8,128)(2,1)S(1)}, u32[]{:S(2)}, u32[]{:S(2)}) %collective-permute-start) | collective-permute-done | bytes 458784 | tf_op jit(solution)/shard_map/cond/branch_0_fun/ppermute | solution.py:473
  16.5 3.2 %collective-permute-done.1.refs_5_.refs_6_.refs_8_ = bf16[1,128,1792]{2,1,0:T(8,128)(2,1)S(1)} collective-permute-done((bf16[1,128,1792]{2,1,0:T(8,128)(2,1)}, bf16[1,128,1792]{2,1,0:T(8,128)(2,1)S(1)}, u32[]{:S(2)}, u32[]{:S(2)}) %collective-permute-start.1) | collective-permute-done | bytes 458784 | tf_op jit(solution)/shard_map/cond/branch_0_fun/ppermute | solution.py:473
  19.7 2.4 %branch_0_fun.6 = (bf16[1,128,1792]{2,1,0:T(8,128)(2,1)S(1)}, bf16[1,128,1792]{2,1,0:T(8,128)(2,1)S(1)}, f32[32,128]{1,0:T(8,128)S(1)}) custom-call(s32[1]{0:T(128)} %bitcast.refs_0_, s32[9]{0:T(128)S(1)} %get-tuple-element.40.refs_1_, bf16[1,128,1792]{2,1,0:T(8,128)(2,1)} %get-tuple-element.128.refs_2_, ...), custom_call_target="tpu_custom_call" | custom-call | flops 352321536 | bytes 4587520 | tf_op jit(solution)/shard_map/cond/branch_0_fun/pallas_call | solution.py:504
  22.2 0.6 %collective-permute-start.4 = (f32[32,128]{1,0:T(8,128)S(1)}, f32[32,128]{1,0:T(8,128)S(1)}, u32[]{:S(2)}, u32[]{:S(2)}) collective-permute-start(f32[32,128]{1,0:T(8,128)S(1)} %get-tuple-element.47.refs_7_), channel_id=1, source_target_pairs={{0,4},{4,0},{8,12},{12,8},{16,20},{20,16},{24,28},{28,24},{1,5},{5... | collective-permute-start | bytes 49160 | tf_op jit(solution)/shard_map/cond/branch_0_fun/ppermute | solution.py:473
  22.7 3.0 %collective-permute-done.2.refs_5_ = bf16[1,128,1792]{2,1,0:T(8,128)(2,1)S(1)} collective-permute-done((bf16[1,128,1792]{2,1,0:T(8,128)(2,1)}, bf16[1,128,1792]{2,1,0:T(8,128)(2,1)S(1)}, u32[]{:S(2)}, u32[]{:S(2)}) %collective-permute-start.2) | collective-permute-done | bytes 458784 | tf_op jit(solution)/shard_map/cond/branch_0_fun/ppermute | solution.py:473
  26.0 1.4 %branch_0_fun.7 = (bf16[1,128,1792]{2,1,0:T(8,128)(2,1)S(1)}, f32[16,128]{1,0:T(8,128)S(1)}) custom-call(s32[1]{0:T(128)} %bitcast.refs_0_, s32[9]{0:T(128)S(1)} %get-tuple-element.40.refs_1_, bf16[1,128,1792]{2,1,0:T(8,128)(2,1)S(1)} %copy-done, bf16[1,128,1792]{2,1,0:T(8,128)(2,1)S(1)} %get-tuple-element.45.refs_3_, ...), custom_call_target="tpu_custom_call" | custom-call | flops 352321536 | bytes 4587520 | tf_op jit(solution)/shard_map/cond/branch_0_fun/pallas_call | solution.py:504
  27.4 1.3 %collective-permute-start.8 = (bf16[1,128,1792]{2,1,0:T(8,128)(2,1)S(1)}, bf16[1,128,1792]{2,1,0:T(8,128)(2,1)S(1)}, u32[]{:S(2)}, u32[]{:S(2)}) collective-permute-start(bf16[1,128,1792]{2,1,0:T(8,128)(2,1)S(1)} %get-tuple-element.55), channel_id=1, source_target_pairs={{8,0},{12,4},{16,8},{20,12},{24,16},{28,20},{9,1},{13,5},{17,9},{2... | collective-permute-start | bytes 1376264 | tf_op jit(solution)/shard_map/cond/branch_0_fun/ppermute | solution.py:473
  28.7 1.6 %branch_0_fun.8.refs_11_.refs_8_ = f32[16,128]{1,0:T(8,128)S(1)} custom-call(s32[1]{0:T(128)} %bitcast.refs_0_, s32[9]{0:T(128)S(1)} %get-tuple-element.40.refs_1_, bf16[1,128,1792]{2,1,0:T(8,128)(2,1)S(1)} %copy-done, bf16[1,128,1792]{2,1,0:T(8,128)(2,1)S(1)} %get-tuple-element.45.refs_3_, bf16[1,128,1792]{2,1,0:T(8,128)(2,1)S(1)} %collective-permute-done.refs_3_.refs_4_, ...), custom_call_target="tpu_custom_call" | custom-call | flops 704643072 | bytes 4587520 | tf_op jit(solution)/shard_map/cond/branch_0_fun/pallas_call | solution.py:504
  30.3 1.7 %collective-permute-start.5 = (f32[16,128]{1,0:T(8,128)S(1)}, f32[16,128]{1,0:T(8,128)S(1)}, u32[]{:S(2)}, u32[]{:S(2)}) collective-permute-start(f32[16,128]{1,0:T(8,128)S(1)} %branch_0_fun.8.refs_11_.refs_8_), channel_id=1, source_target_pairs={{0,4},{4,0},{8,12},{12,8},{16,20},{20,16},{24,28},{28,24},{1,5},{5... | collective-permute-start | bytes 24584 | tf_op jit(solution)/shard_map/cond/branch_0_fun/ppermute | solution.py:473
  32.0 1.4 %branch_0_fun.11 = bf16[1,128,1792]{2,1,0:T(8,128)(2,1)S(1)} custom-call(s32[1]{0:T(128)} %bitcast.refs_0_, s32[9]{0:T(128)S(1)} %get-tuple-element.40.refs_1_, bf16[1,128,1792]{2,1,0:T(8,128)(2,1)S(1)} %copy-done, bf16[1,128,1792]{2,1,0:T(8,128)(2,1)S(1)} %get-tuple-element.45.refs_3_, bf16[1,128,1792]{2,1,0:T(8,128)(2,1)S(1)} %collective-permute-done.refs_3_.refs_4_, ...), custom_call_target="tpu_custom_call" | custom-call | flops 352321536 | bytes 4587520 | tf_op jit(solution)/shard_map/cond/branch_0_fun/pallas_call | solution.py:504
  33.4 0.6 %collective-permute-done.5.refs_12_ = f32[16,128]{1,0:T(8,128)S(1)} collective-permute-done((f32[16,128]{1,0:T(8,128)S(1)}, f32[16,128]{1,0:T(8,128)S(1)}, u32[]{:S(2)}, u32[]{:S(2)}) %collective-permute-start.5) | collective-permute-done | bytes 8224 | tf_op jit(solution)/shard_map/cond/branch_0_fun/ppermute | solution.py:473
  34.0 2.5 %branch_0_fun.9 = (bf16[1,128,1792]{2,1,0:T(8,128)(2,1)S(1)}, bf16[1,128,1792]{2,1,0:T(8,128)(2,1)S(1)}, bf16[1,128,1792]{2,1,0:T(8,128)(2,1)S(1)}, bf16[1,128,1792]{2,1,0:T(8,128)(2,1)S(1)}) custom-call(s32[1]{0:T(128)} %bitcast.refs_0_, s32[9]{0:T(128)S(1)} %get-tuple-element.40.refs_1_, bf16[1,128,1792]{2,1,0:T(8,128)(2,1)S(1)} %copy-done, ...), custom_call_target="tpu_custom_call" | custom-call | flops 1409286144 | bytes 4587520 | tf_op jit(solution)/shard_map/cond/branch_0_fun/pallas_call | solution.py:504
  36.6 1.3 %collective-permute-start.6 = (bf16[1,128,1792]{2,1,0:T(8,128)(2,1)S(1)}, bf16[1,128,1792]{2,1,0:T(8,128)(2,1)S(1)}, u32[]{:S(2)}, u32[]{:S(2)}) collective-permute-start(bf16[1,128,1792]{2,1,0:T(8,128)(2,1)S(1)} %get-tuple-element.50), channel_id=1, source_target_pairs={{8,0},{12,4},{16,8},{20,12},{24,16},{28,20},{9,1},{13,5},{17,9},{2... | collective-permute-start | bytes 1376264 | tf_op jit(solution)/shard_map/cond/branch_0_fun/ppermute | solution.py:473
  37.9 1.7 %collective-permute-start.7 = (bf16[1,128,1792]{2,1,0:T(8,128)(2,1)S(1)}, bf16[1,128,1792]{2,1,0:T(8,128)(2,1)S(1)}, u32[]{:S(2)}, u32[]{:S(2)}) collective-permute-start(bf16[1,128,1792]{2,1,0:T(8,128)(2,1)S(1)} %get-tuple-element.52), channel_id=1, source_target_pairs={{0,4},{4,0},{8,12},{12,8},{16,20},{20,16},{24,28},{28,24},{1,5},{5... | collective-permute-start | bytes 1376264 | tf_op jit(solution)/shard_map/cond/branch_0_fun/ppermute | solution.py:473
  39.6 2.4 %collective-permute-done.8 = bf16[1,128,1792]{2,1,0:T(8,128)(2,1)S(1)} collective-permute-done((bf16[1,128,1792]{2,1,0:T(8,128)(2,1)S(1)}, bf16[1,128,1792]{2,1,0:T(8,128)(2,1)S(1)}, u32[]{:S(2)}, u32[]{:S(2)}) %collective-permute-start.8) | collective-permute-done | bytes 458784 | tf_op jit(solution)/shard_map/cond/branch_0_fun/ppermute | solution.py:473
  41.9 0.9 %convert_add_fusion = bf16[1,128,1792]{2,1,0:T(8,128)(2,1)} fusion(bf16[1,128,1792]{2,1,0:T(8,128)(2,1)S(1)} %collective-permute-done.8, bf16[1,128,1792]{2,1,0:T(8,128)(2,1)S(1)} %branch_0_fun.11), kind=kLoop, calls=%fused_computation | loop fusion | flops 917504 | bytes 1376256 | tf_op jit(solution)/shard_map/cond/branch_0_fun/add | solution.py:580
  42.8 7.9 %collective-permute-done.6.refs_1_ = bf16[1,128,1792]{2,1,0:T(8,128)(2,1)S(1)} collective-permute-done((bf16[1,128,1792]{2,1,0:T(8,128)(2,1)S(1)}, bf16[1,128,1792]{2,1,0:T(8,128)(2,1)S(1)}, u32[]{:S(2)}, u32[]{:S(2)}) %collective-permute-start.6) | collective-permute-done | bytes 458784 | tf_op jit(solution)/shard_map/cond/branch_0_fun/ppermute | solution.py:473
  50.7 1.1 %branch_0_fun.10 = (bf16[1,128,1792]{2,1,0:T(8,128)(2,1)}, bf16[1,128,1792]{2,1,0:T(8,128)(2,1)}) custom-call(bf16[1,128,1792]{2,1,0:T(8,128)(2,1)S(1)} %get-tuple-element.49.refs_0_, bf16[1,128,1792]{2,1,0:T(8,128)(2,1)S(1)} %collective-permute-done.6.refs_1_, bf16[1,128,1792]{2,1,0:T(8,128)(2,1)S(1)} %get-tuple-element.51.refs_2_, ...), custom_call_target="tpu_custom_call" | custom-call | bytes 4587520 | tf_op jit(solution)/shard_map/cond/branch_0_fun/pallas_call | solution.py:504
  (7 shorter events, 0.3 us)
Async XLA Ops:
  2.0 14.6 %collective-permute-start = (bf16[1,128,1792]{2,1,0:T(8,128)(2,1)}, bf16[1,128,1792]{2,1,0:T(8,128)(2,1)S(1)}, u32[]{:S(2)}, u32[]{:S(2)}) collective-permute-start(bf16[1,128,1792]{2,1,0:T(8,128)(2,1)} %get-tuple-element.128.refs_2_), channel_id=1, source_target_pairs={{0,4},{4,0},{8,12},{12,8},{16,20},{20,16},{24,28},{28,24},{1,5},{5... | collective-permute-start | bytes 1376264 | tf_op jit(solution)/shard_map/cond/branch_0_fun/ppermute | solution.py:473
  5.0 14.7 %collective-permute-start.1 = (bf16[1,128,1792]{2,1,0:T(8,128)(2,1)}, bf16[1,128,1792]{2,1,0:T(8,128)(2,1)S(1)}, u32[]{:S(2)}, u32[]{:S(2)}) collective-permute-start(bf16[1,128,1792]{2,1,0:T(8,128)(2,1)} %get-tuple-element.131.refs_4_.refs_6_), channel_id=1, source_target_pairs={{0,8},{4,12},{8,16},{12,20},{16,24},{20,28},{1,9},{5,13},{9,17},{1... | collective-permute-start | bytes 1376264 | tf_op jit(solution)/shard_map/cond/branch_0_fun/ppermute | solution.py:473
  8.5 17.2 %collective-permute-start.2 = (bf16[1,128,1792]{2,1,0:T(8,128)(2,1)}, bf16[1,128,1792]{2,1,0:T(8,128)(2,1)S(1)}, u32[]{:S(2)}, u32[]{:S(2)}) collective-permute-start(bf16[1,128,1792]{2,1,0:T(8,128)(2,1)} %get-tuple-element.134.refs_6_), channel_id=1, source_target_pairs={{0,4},{4,0},{8,12},{12,8},{16,20},{20,16},{24,28},{28,24},{1,5},{5... | collective-permute-start | bytes 1376264 | tf_op jit(solution)/shard_map/cond/branch_0_fun/ppermute | solution.py:473
  9.1 19.6 %collective-permute-start.3 = (bf16[1,128,1792]{2,1,0:T(8,128)(2,1)}, bf16[1,128,1792]{2,1,0:T(8,128)(2,1)S(1)}, u32[]{:S(2)}, u32[]{:S(2)}) collective-permute-start(bf16[1,128,1792]{2,1,0:T(8,128)(2,1)} %get-tuple-element.137.refs_7_), channel_id=1, source_target_pairs={{0,8},{4,12},{8,16},{12,20},{16,24},{20,28},{24,0},{28,4},{1,9},{5... | collective-permute-start | bytes 1376264 | tf_op jit(solution)/shard_map/cond/branch_0_fun/ppermute | solution.py:473
  19.7 6.3 %copy-start = (bf16[1,128,1792]{2,1,0:T(8,128)(2,1)S(1)}, bf16[1,128,1792]{2,1,0:T(8,128)(2,1)}, u32[]{:S(2)}) copy-start(bf16[1,128,1792]{2,1,0:T(8,128)(2,1)} %get-tuple-element.128.refs_2_) | copy-start | bytes 1376260
  22.2 3.8 %collective-permute-start.4 = (f32[32,128]{1,0:T(8,128)S(1)}, f32[32,128]{1,0:T(8,128)S(1)}, u32[]{:S(2)}, u32[]{:S(2)}) collective-permute-start(f32[32,128]{1,0:T(8,128)S(1)} %get-tuple-element.47.refs_7_), channel_id=1, source_target_pairs={{0,4},{4,0},{8,12},{12,8},{16,20},{20,16},{24,28},{28,24},{1,5},{5... | collective-permute-start | bytes 49160 | tf_op jit(solution)/shard_map/cond/branch_0_fun/ppermute | solution.py:473
  26.0 2.7 %copy-start.3 = (bf16[1,128,1792]{2,1,0:T(8,128)(2,1)S(1)}, bf16[1,128,1792]{2,1,0:T(8,128)(2,1)}, u32[]{:S(2)}) copy-start(bf16[1,128,1792]{2,1,0:T(8,128)(2,1)} %get-tuple-element.131.refs_4_.refs_6_) | copy-start | bytes 1376260
  27.4 14.6 %collective-permute-start.8 = (bf16[1,128,1792]{2,1,0:T(8,128)(2,1)S(1)}, bf16[1,128,1792]{2,1,0:T(8,128)(2,1)S(1)}, u32[]{:S(2)}, u32[]{:S(2)}) collective-permute-start(bf16[1,128,1792]{2,1,0:T(8,128)(2,1)S(1)} %get-tuple-element.55), channel_id=1, source_target_pairs={{8,0},{12,4},{16,8},{20,12},{24,16},{28,20},{9,1},{13,5},{17,9},{2... | collective-permute-start | bytes 1376264 | tf_op jit(solution)/shard_map/cond/branch_0_fun/ppermute | solution.py:473
  30.3 3.7 %collective-permute-start.5 = (f32[16,128]{1,0:T(8,128)S(1)}, f32[16,128]{1,0:T(8,128)S(1)}, u32[]{:S(2)}, u32[]{:S(2)}) collective-permute-start(f32[16,128]{1,0:T(8,128)S(1)} %branch_0_fun.8.refs_11_.refs_8_), channel_id=1, source_target_pairs={{0,4},{4,0},{8,12},{12,8},{16,20},{20,16},{24,28},{28,24},{1,5},{5... | collective-permute-start | bytes 24584 | tf_op jit(solution)/shard_map/cond/branch_0_fun/ppermute | solution.py:473
  36.6 14.2 %collective-permute-start.6 = (bf16[1,128,1792]{2,1,0:T(8,128)(2,1)S(1)}, bf16[1,128,1792]{2,1,0:T(8,128)(2,1)S(1)}, u32[]{:S(2)}, u32[]{:S(2)}) collective-permute-start(bf16[1,128,1792]{2,1,0:T(8,128)(2,1)S(1)} %get-tuple-element.50), channel_id=1, source_target_pairs={{8,0},{12,4},{16,8},{20,12},{24,16},{28,20},{9,1},{13,5},{17,9},{2... | collective-permute-start | bytes 1376264 | tf_op jit(solution)/shard_map/cond/branch_0_fun/ppermute | solution.py:473
  37.9 12.9 %collective-permute-start.7 = (bf16[1,128,1792]{2,1,0:T(8,128)(2,1)S(1)}, bf16[1,128,1792]{2,1,0:T(8,128)(2,1)S(1)}, u32[]{:S(2)}, u32[]{:S(2)}) collective-permute-start(bf16[1,128,1792]{2,1,0:T(8,128)(2,1)S(1)} %get-tuple-element.52), channel_id=1, source_target_pairs={{0,4},{4,0},{8,12},{12,8},{16,20},{20,16},{24,28},{28,24},{1,5},{5... | collective-permute-start | bytes 1376264 | tf_op jit(solution)/shard_map/cond/branch_0_fun/ppermute | solution.py:473

commit v3 on v1

--- a/solution.py
+++ b/solution.py
@@ -486,15 +486,15 @@
         columns = {*range(len(lead), len(lead) + len(wides)), *range(inputs, inputs + outs)}
 
         def body(*refs):
-            def half(step, carry):
-                cut = pl.ds(pl.multiple_of(step * part, LANES), part)
+            def half(step):
+                cut = pl.ds(step * part, part)
                 views = [ref.at[:, :, cut] if n in columns else ref for n, ref in enumerate(refs)]
                 if not plain:
                     views[0] = (refs[0][0], step)
                 kernel(*views)
-                return carry
-
-            lax.fori_loop(0, steps, half, 0)
+
+            for step in range(steps):
+                half(step)
 
         return pl.pallas_call(
             body,

time: 73.9 us -> 52 us (0.70)
  the two profiles are of different devices: /device:TPU:16 before, /device:TPU:0 now
where the time goes in v3:
time: 52 us; the launch traced here: 51.8 us
  waiting for transfers between devices  23.1 us (44%)
  starting transfers between devices  15.3 us (29%)
  Pallas kernels  11.7 us (22%)
  other arithmetic  0.91 us (2%)
  between operations  0.67 us (1%)
    ppermute x9, waiting for transfers between devices, send(): return lax.ppermute(value, 'seq', pairs)  23.1 us
    ppermute x9, starting transfers between devices, send(): return lax.ppermute(value, 'seq', pairs)  15.3 us
    pallas_call x6, Pallas kernels, call(): pl.pallas_call(body, in_specs=[smem] * len(lead) + [vmem] * (len(wides) +...  10.4 us
    pallas_call x1, Pallas kernels, program_facts(): pl.pallas_call(functools.partial(program_kernel, rows.bit_length() - 1),...  1.29 us
  transfers between devices with their start and end apart: 9, of which 7 were waited for; matrix products, arithmetic and copies ran while one was open for 2% of the time, Pallas kernels for 18%

profile of v3, /device:TPU:0, one launch (start us, length us, event | category | flops | bytes accessed | tf_op | source)
XLA Modules:
  0.0 51.8 jit_solution(129002990516203938)
XLA Ops:
  0.6 1.3 %shard_map.91 = s32[9]{0:T(128)S(1)} custom-call(s32[8]{0:T(128)} %lengths_ref.1), custom_call_target="tpu_custom_call" | custom-call | tf_op jit(solution)/shard_map/pallas_call | solution.py:596
  2.0 49.8 %conditional.4 = (bf16[1,128,1792]{2,1,0:T(8,128)(2,1)}, bf16[1,128,1792]{2,1,0:T(8,128)(2,1)}, bf16[1,128,1792]{2,1,0:T(8,128)(2,1)}) conditional(s32[]{:T(128)} %bitcast.3, (bf16[1,128,1792]{2,1,0:T(8,128)(2,1)}, bf16[1,128,1792]{2,1,0:T(8,128)(2,1)}, s32[9]{0:T(128)S(1)}, bf16[1,128,1792]{2,1,0:T(8,128)(2,1)}, ...), branch_computations={%region_0.0_spmd, %region_1.0_spmd, %region_2.0_spmd} | conditional | flops 4228775936 | bytes 55903040
  2.0 3.0 %collective-permute-start = (bf16[1,128,1792]{2,1,0:T(8,128)(2,1)}, bf16[1,128,1792]{2,1,0:T(8,128)(2,1)S(1)}, u32[]{:S(2)}, u32[]{:S(2)}) collective-permute-start(bf16[1,128,1792]{2,1,0:T(8,128)(2,1)} %get-tuple-element.128.refs_2_), channel_id=1, source_target_pairs={{0,4},{4,0},{8,12},{12,8},{16,20},{20,16},{24,28},{28,24},{1,5},{5... | collective-permute-start | bytes 1376264 | tf_op jit(solution)/shard_map/cond/branch_0_fun/ppermute | solution.py:473
  5.0 3.5 %collective-permute-start.1 = (bf16[1,128,1792]{2,1,0:T(8,128)(2,1)}, bf16[1,128,1792]{2,1,0:T(8,128)(2,1)S(1)}, u32[]{:S(2)}, u32[]{:S(2)}) collective-permute-start(bf16[1,128,1792]{2,1,0:T(8,128)(2,1)} %get-tuple-element.131.refs_4_.refs_6_), channel_id=1, source_target_pairs={{0,8},{4,12},{8,16},{12,20},{16,24},{20,28},{1,9},{5,13},{9,17},{1... | collective-permute-start | bytes 1376264 | tf_op jit(solution)/shard_map/cond/branch_0_fun/ppermute | solution.py:473
  8.5 0.6 %collective-permute-start.2 = (bf16[1,128,1792]{2,1,0:T(8,128)(2,1)}, bf16[1,128,1792]{2,1,0:T(8,128)(2,1)S(1)}, u32[]{:S(2)}, u32[]{:S(2)}) collective-permute-start(bf16[1,128,1792]{2,1,0:T(8,128)(2,1)} %get-tuple-element.134.refs_6_), channel_id=1, source_target_pairs={{0,4},{4,0},{8,12},{12,8},{16,20},{20,16},{24,28},{28,24},{1,5},{5... | collective-permute-start | bytes 1376264 | tf_op jit(solution)/shard_map/cond/branch_0_fun/ppermute | solution.py:473
  9.1 1.6 %collective-permute-start.3 = (bf16[1,128,1792]{2,1,0:T(8,128)(2,1)}, bf16[1,128,1792]{2,1,0:T(8,128)(2,1)S(1)}, u32[]{:S(2)}, u32[]{:S(2)}) collective-permute-start(bf16[1,128,1792]{2,1,0:T(8,128)(2,1)} %get-tuple-element.137.refs_7_), channel_id=1, source_target_pairs={{0,8},{4,12},{8,16},{12,20},{16,24},{20,28},{24,0},{28,4},{1,9},{5... | collective-permute-start | bytes 1376264 | tf_op jit(solution)/shard_map/cond/branch_0_fun/ppermute | solution.py:473
  10.6 5.9 %collective-permute-done.refs_3_.refs_4_ = bf16[1,128,1792]{2,1,0:T(8,128)(2,1)S(1)} collective-permute-done((bf16[1,128,1792]{2,1,0:T(8,128)(2,1)}, bf16[1,128,1792]{2,1,0:T(8,128)(2,1)S(1)}, u32[]{:S(2)}, u32[]{:S(2)}) %collective-permute-start) | collective-permute-done | bytes 458784 | tf_op jit(solution)/shard_map/cond/branch_0_fun/ppermute | solution.py:473
  16.5 3.2 %collective-permute-done.1.refs_5_.refs_6_.refs_8_ = bf16[1,128,1792]{2,1,0:T(8,128)(2,1)S(1)} collective-permute-done((bf16[1,128,1792]{2,1,0:T(8,128)(2,1)}, bf16[1,128,1792]{2,1,0:T(8,128)(2,1)S(1)}, u32[]{:S(2)}, u32[]{:S(2)}) %collective-permute-start.1) | collective-permute-done | bytes 458784 | tf_op jit(solution)/shard_map/cond/branch_0_fun/ppermute | solution.py:473
  19.7 2.4 %branch_0_fun.6 = (bf16[1,128,1792]{2,1,0:T(8,128)(2,1)S(1)}, bf16[1,128,1792]{2,1,0:T(8,128)(2,1)S(1)}, f32[32,128]{1,0:T(8,128)S(1)}) custom-call(s32[1]{0:T(128)} %bitcast.refs_0_, s32[9]{0:T(128)S(1)} %get-tuple-element.40.refs_1_, bf16[1,128,1792]{2,1,0:T(8,128)(2,1)} %get-tuple-element.128.refs_2_, ...), custom_call_target="tpu_custom_call" | custom-call | flops 352321536 | bytes 4587520 | tf_op jit(solution)/shard_map/cond/branch_0_fun/pallas_call | solution.py:499
  22.2 0.6 %collective-permute-start.4 = (f32[32,128]{1,0:T(8,128)S(1)}, f32[32,128]{1,0:T(8,128)S(1)}, u32[]{:S(2)}, u32[]{:S(2)}) collective-permute-start(f32[32,128]{1,0:T(8,128)S(1)} %get-tuple-element.47.refs_7_), channel_id=1, source_target_pairs={{0,4},{4,0},{8,12},{12,8},{16,20},{20,16},{24,28},{28,24},{1,5},{5... | collective-permute-start | bytes 49160 | tf_op jit(solution)/shard_map/cond/branch_0_fun/ppermute | solution.py:473
  22.7 3.0 %collective-permute-done.2.refs_5_ = bf16[1,128,1792]{2,1,0:T(8,128)(2,1)S(1)} collective-permute-done((bf16[1,128,1792]{2,1,0:T(8,128)(2,1)}, bf16[1,128,1792]{2,1,0:T(8,128)(2,1)S(1)}, u32[]{:S(2)}, u32[]{:S(2)}) %collective-permute-start.2) | collective-permute-done | bytes 458784 | tf_op jit(solution)/shard_map/cond/branch_0_fun/ppermute | solution.py:473
  26.0 1.4 %branch_0_fun.7 = (bf16[1,128,1792]{2,1,0:T(8,128)(2,1)S(1)}, f32[16,128]{1,0:T(8,128)S(1)}) custom-call(s32[1]{0:T(128)} %bitcast.refs_0_, s32[9]{0:T(128)S(1)} %get-tuple-element.40.refs_1_, bf16[1,128,1792]{2,1,0:T(8,128)(2,1)S(1)} %copy-done, bf16[1,128,1792]{2,1,0:T(8,128)(2,1)S(1)} %get-tuple-element.45.refs_3_, ...), custom_call_target="tpu_custom_call" | custom-call | flops 352321536 | bytes 4587520 | tf_op jit(solution)/shard_map/cond/branch_0_fun/pallas_call | solution.py:499
  27.4 1.3 %collective-permute-start.8 = (bf16[1,128,1792]{2,1,0:T(8,128)(2,1)S(1)}, bf16[1,128,1792]{2,1,0:T(8,128)(2,1)S(1)}, u32[]{:S(2)}, u32[]{:S(2)}) collective-permute-start(bf16[1,128,1792]{2,1,0:T(8,128)(2,1)S(1)} %get-tuple-element.55), channel_id=1, source_target_pairs={{8,0},{12,4},{16,8},{20,12},{24,16},{28,20},{9,1},{13,5},{17,9},{2... | collective-permute-start | bytes 1376264 | tf_op jit(solution)/shard_map/cond/branch_0_fun/ppermute | solution.py:473
  28.7 1.6 %branch_0_fun.8.refs_11_.refs_8_ = f32[16,128]{1,0:T(8,128)S(1)} custom-call(s32[1]{0:T(128)} %bitcast.refs_0_, s32[9]{0:T(128)S(1)} %get-tuple-element.40.refs_1_, bf16[1,128,1792]{2,1,0:T(8,128)(2,1)S(1)} %copy-done, bf16[1,128,1792]{2,1,0:T(8,128)(2,1)S(1)} %get-tuple-element.45.refs_3_, bf16[1,128,1792]{2,1,0:T(8,128)(2,1)S(1)} %collective-permute-done.refs_3_.refs_4_, ...), custom_call_target="tpu_custom_call" | custom-call | flops 704643072 | bytes 4587520 | tf_op jit(solution)/shard_map/cond/branch_0_fun/pallas_call | solution.py:499
  30.3 1.7 %collective-permute-start.5 = (f32[16,128]{1,0:T(8,128)S(1)}, f32[16,128]{1,0:T(8,128)S(1)}, u32[]{:S(2)}, u32[]{:S(2)}) collective-permute-start(f32[16,128]{1,0:T(8,128)S(1)} %branch_0_fun.8.refs_11_.refs_8_), channel_id=1, source_target_pairs={{0,4},{4,0},{8,12},{12,8},{16,20},{20,16},{24,28},{28,24},{1,5},{5... | collective-permute-start | bytes 24584 | tf_op jit(solution)/shard_map/cond/branch_0_fun/ppermute | solution.py:473
  32.0 1.4 %branch_0_fun.11 = bf16[1,128,1792]{2,1,0:T(8,128)(2,1)S(1)} custom-call(s32[1]{0:T(128)} %bitcast.refs_0_, s32[9]{0:T(128)S(1)} %get-tuple-element.40.refs_1_, bf16[1,128,1792]{2,1,0:T(8,128)(2,1)S(1)} %copy-done, bf16[1,128,1792]{2,1,0:T(8,128)(2,1)S(1)} %get-tuple-element.45.refs_3_, bf16[1,128,1792]{2,1,0:T(8,128)(2,1)S(1)} %collective-permute-done.refs_3_.refs_4_, ...), custom_call_target="tpu_custom_call" | custom-call | flops 352321536 | bytes 4587520 | tf_op jit(solution)/shard_map/cond/branch_0_fun/pallas_call | solution.py:499
  33.4 0.6 %collective-permute-done.5.refs_12_ = f32[16,128]{1,0:T(8,128)S(1)} collective-permute-done((f32[16,128]{1,0:T(8,128)S(1)}, f32[16,128]{1,0:T(8,128)S(1)}, u32[]{:S(2)}, u32[]{:S(2)}) %collective-permute-start.5) | collective-permute-done | bytes 8224 | tf_op jit(solution)/shard_map/cond/branch_0_fun/ppermute | solution.py:473
  34.0 2.5 %branch_0_fun.9 = (bf16[1,128,1792]{2,1,0:T(8,128)(2,1)S(1)}, bf16[1,128,1792]{2,1,0:T(8,128)(2,1)S(1)}, bf16[1,128,1792]{2,1,0:T(8,128)(2,1)S(1)}, bf16[1,128,1792]{2,1,0:T(8,128)(2,1)S(1)}) custom-call(s32[1]{0:T(128)} %bitcast.refs_0_, s32[9]{0:T(128)S(1)} %get-tuple-element.40.refs_1_, bf16[1,128,1792]{2,1,0:T(8,128)(2,1)S(1)} %copy-done, ...), custom_call_target="tpu_custom_call" | custom-call | flops 1409286144 | bytes 4587520 | tf_op jit(solution)/shard_map/cond/branch_0_fun/pallas_call | solution.py:499
  36.6 1.3 %collective-permute-start.6 = (bf16[1,128,1792]{2,1,0:T(8,128)(2,1)S(1)}, bf16[1,128,1792]{2,1,0:T(8,128)(2,1)S(1)}, u32[]{:S(2)}, u32[]{:S(2)}) collective-permute-start(bf16[1,128,1792]{2,1,0:T(8,128)(2,1)S(1)} %get-tuple-element.50), channel_id=1, source_target_pairs={{8,0},{12,4},{16,8},{20,12},{24,16},{28,20},{9,1},{13,5},{17,9},{2... | collective-permute-start | bytes 1376264 | tf_op jit(solution)/shard_map/cond/branch_0_fun/ppermute | solution.py:473
  37.9 1.7 %collective-permute-start.7 = (bf16[1,128,1792]{2,1,0:T(8,128)(2,1)S(1)}, bf16[1,128,1792]{2,1,0:T(8,128)(2,1)S(1)}, u32[]{:S(2)}, u32[]{:S(2)}) collective-permute-start(bf16[1,128,1792]{2,1,0:T(8,128)(2,1)S(1)} %get-tuple-element.52), channel_id=1, source_target_pairs={{0,4},{4,0},{8,12},{12,8},{16,20},{20,16},{24,28},{28,24},{1,5},{5... | collective-permute-start | bytes 1376264 | tf_op jit(solution)/shard_map/cond/branch_0_fun/ppermute | solution.py:473
  39.6 2.4 %collective-permute-done.8 = bf16[1,128,1792]{2,1,0:T(8,128)(2,1)S(1)} collective-permute-done((bf16[1,128,1792]{2,1,0:T(8,128)(2,1)S(1)}, bf16[1,128,1792]{2,1,0:T(8,128)(2,1)S(1)}, u32[]{:S(2)}, u32[]{:S(2)}) %collective-permute-start.8) | collective-permute-done | bytes 458784 | tf_op jit(solution)/shard_map/cond/branch_0_fun/ppermute | solution.py:473
  41.9 0.9 %convert_add_fusion = bf16[1,128,1792]{2,1,0:T(8,128)(2,1)} fusion(bf16[1,128,1792]{2,1,0:T(8,128)(2,1)S(1)} %collective-permute-done.8, bf16[1,128,1792]{2,1,0:T(8,128)(2,1)S(1)} %branch_0_fun.11), kind=kLoop, calls=%fused_computation | loop fusion | flops 917504 | bytes 1376256 | tf_op jit(solution)/shard_map/cond/branch_0_fun/add | solution.py:575
  42.8 7.9 %collective-permute-done.6.refs_1_ = bf16[1,128,1792]{2,1,0:T(8,128)(2,1)S(1)} collective-permute-done((bf16[1,128,1792]{2,1,0:T(8,128)(2,1)S(1)}, bf16[1,128,1792]{2,1,0:T(8,128)(2,1)S(1)}, u32[]{:S(2)}, u32[]{:S(2)}) %collective-permute-start.6) | collective-permute-done | bytes 458784 | tf_op jit(solution)/shard_map/cond/branch_0_fun/ppermute | solution.py:473
  50.7 1.1 %branch_0_fun.10 = (bf16[1,128,1792]{2,1,0:T(8,128)(2,1)}, bf16[1,128,1792]{2,1,0:T(8,128)(2,1)}) custom-call(bf16[1,128,1792]{2,1,0:T(8,128)(2,1)S(1)} %get-tuple-element.49.refs_0_, bf16[1,128,1792]{2,1,0:T(8,128)(2,1)S(1)} %collective-permute-done.6.refs_1_, bf16[1,128,1792]{2,1,0:T(8,128)(2,1)S(1)} %get-tuple-element.51.refs_2_, ...), custom_call_target="tpu_custom_call" | custom-call | bytes 4587520 | tf_op jit(solution)/shard_map/cond/branch_0_fun/pallas_call | solution.py:499
  (7 shorter events, 0.3 us)
Async XLA Ops:
  2.0 14.6 %collective-permute-start = (bf16[1,128,1792]{2,1,0:T(8,128)(2,1)}, bf16[1,128,1792]{2,1,0:T(8,128)(2,1)S(1)}, u32[]{:S(2)}, u32[]{:S(2)}) collective-permute-start(bf16[1,128,1792]{2,1,0:T(8,128)(2,1)} %get-tuple-element.128.refs_2_), channel_id=1, source_target_pairs={{0,4},{4,0},{8,12},{12,8},{16,20},{20,16},{24,28},{28,24},{1,5},{5... | collective-permute-start | bytes 1376264 | tf_op jit(solution)/shard_map/cond/branch_0_fun/ppermute | solution.py:473
  5.0 14.7 %collective-permute-start.1 = (bf16[1,128,1792]{2,1,0:T(8,128)(2,1)}, bf16[1,128,1792]{2,1,0:T(8,128)(2,1)S(1)}, u32[]{:S(2)}, u32[]{:S(2)}) collective-permute-start(bf16[1,128,1792]{2,1,0:T(8,128)(2,1)} %get-tuple-element.131.refs_4_.refs_6_), channel_id=1, source_target_pairs={{0,8},{4,12},{8,16},{12,20},{16,24},{20,28},{1,9},{5,13},{9,17},{1... | collective-permute-start | bytes 1376264 | tf_op jit(solution)/shard_map/cond/branch_0_fun/ppermute | solution.py:473
  8.5 17.2 %collective-permute-start.2 = (bf16[1,128,1792]{2,1,0:T(8,128)(2,1)}, bf16[1,128,1792]{2,1,0:T(8,128)(2,1)S(1)}, u32[]{:S(2)}, u32[]{:S(2)}) collective-permute-start(bf16[1,128,1792]{2,1,0:T(8,128)(2,1)} %get-tuple-element.134.refs_6_), channel_id=1, source_target_pairs={{0,4},{4,0},{8,12},{12,8},{16,20},{20,16},{24,28},{28,24},{1,5},{5... | collective-permute-start | bytes 1376264 | tf_op jit(solution)/shard_map/cond/branch_0_fun/ppermute | solution.py:473
  9.1 19.6 %collective-permute-start.3 = (bf16[1,128,1792]{2,1,0:T(8,128)(2,1)}, bf16[1,128,1792]{2,1,0:T(8,128)(2,1)S(1)}, u32[]{:S(2)}, u32[]{:S(2)}) collective-permute-start(bf16[1,128,1792]{2,1,0:T(8,128)(2,1)} %get-tuple-element.137.refs_7_), channel_id=1, source_target_pairs={{0,8},{4,12},{8,16},{12,20},{16,24},{20,28},{24,0},{28,4},{1,9},{5... | collective-permute-start | bytes 1376264 | tf_op jit(solution)/shard_map/cond/branch_0_fun/ppermute | solution.py:473
  19.7 6.3 %copy-start = (bf16[1,128,1792]{2,1,0:T(8,128)(2,1)S(1)}, bf16[1,128,1792]{2,1,0:T(8,128)(2,1)}, u32[]{:S(2)}) copy-start(bf16[1,128,1792]{2,1,0:T(8,128)(2,1)} %get-tuple-element.128.refs_2_) | copy-start | bytes 1376260
  22.2 3.8 %collective-permute-start.4 = (f32[32,128]{1,0:T(8,128)S(1)}, f32[32,128]{1,0:T(8,128)S(1)}, u32[]{:S(2)}, u32[]{:S(2)}) collective-permute-start(f32[32,128]{1,0:T(8,128)S(1)} %get-tuple-element.47.refs_7_), channel_id=1, source_target_pairs={{0,4},{4,0},{8,12},{12,8},{16,20},{20,16},{24,28},{28,24},{1,5},{5... | collective-permute-start | bytes 49160 | tf_op jit(solution)/shard_map/cond/branch_0_fun/ppermute | solution.py:473
  26.0 2.7 %copy-start.3 = (bf16[1,128,1792]{2,1,0:T(8,128)(2,1)S(1)}, bf16[1,128,1792]{2,1,0:T(8,128)(2,1)}, u32[]{:S(2)}) copy-start(bf16[1,128,1792]{2,1,0:T(8,128)(2,1)} %get-tuple-element.131.refs_4_.refs_6_) | copy-start | bytes 1376260
  27.4 14.6 %collective-permute-start.8 = (bf16[1,128,1792]{2,1,0:T(8,128)(2,1)S(1)}, bf16[1,128,1792]{2,1,0:T(8,128)(2,1)S(1)}, u32[]{:S(2)}, u32[]{:S(2)}) collective-permute-start(bf16[1,128,1792]{2,1,0:T(8,128)(2,1)S(1)} %get-tuple-element.55), channel_id=1, source_target_pairs={{8,0},{12,4},{16,8},{20,12},{24,16},{28,20},{9,1},{13,5},{17,9},{2... | collective-permute-start | bytes 1376264 | tf_op jit(solution)/shard_map/cond/branch_0_fun/ppermute | solution.py:473
  30.3 3.7 %collective-permute-start.5 = (f32[16,128]{1,0:T(8,128)S(1)}, f32[16,128]{1,0:T(8,128)S(1)}, u32[]{:S(2)}, u32[]{:S(2)}) collective-permute-start(f32[16,128]{1,0:T(8,128)S(1)} %branch_0_fun.8.refs_11_.refs_8_), channel_id=1, source_target_pairs={{0,4},{4,0},{8,12},{12,8},{16,20},{20,16},{24,28},{28,24},{1,5},{5... | collective-permute-start | bytes 24584 | tf_op jit(solution)/shard_map/cond/branch_0_fun/ppermute | solution.py:473
  36.6 14.2 %collective-permute-start.6 = (bf16[1,128,1792]{2,1,0:T(8,128)(2,1)S(1)}, bf16[1,128,1792]{2,1,0:T(8,128)(2,1)S(1)}, u32[]{:S(2)}, u32[]{:S(2)}) collective-permute-start(bf16[1,128,1792]{2,1,0:T(8,128)(2,1)S(1)} %get-tuple-element.50), channel_id=1, source_target_pairs={{8,0},{12,4},{16,8},{20,12},{24,16},{28,20},{9,1},{13,5},{17,9},{2... | collective-permute-start | bytes 1376264 | tf_op jit(solution)/shard_map/cond/branch_0_fun/ppermute | solution.py:473
  37.9 12.9 %collective-permute-start.7 = (bf16[1,128,1792]{2,1,0:T(8,128)(2,1)S(1)}, bf16[1,128,1792]{2,1,0:T(8,128)(2,1)S(1)}, u32[]{:S(2)}, u32[]{:S(2)}) collective-permute-start(bf16[1,128,1792]{2,1,0:T(8,128)(2,1)S(1)} %get-tuple-element.52), channel_id=1, source_target_pairs={{0,4},{4,0},{8,12},{12,8},{16,20},{20,16},{24,28},{28,24},{1,5},{5... | collective-permute-start | bytes 1376264 | tf_op jit(solution)/shard_map/cond/branch_0_fun/ppermute | solution.py:473
